TPU v7x, 512 devices: a whole 4x4x16 slice. The times are simulated.
512 devices in a mesh: day: 64 (over z, y), pair: 8 (over x, core).
Axes of the slice: x: 4, y: 4, z: 16, core: 2. Of those that a mesh axis runs over, the one named last changes fastest.
Arguments:
- spectra: bfloat16 [128, 128, 4096], P('day', 'pair'), may hold values from -40 to 40
- pair_stations: int32 [512, 2], P('pair'), may hold values from 0 to 127
- availability: int32 [128, 128], P('day'), may hold values from 0 to 1
Outputs:
- stacks: bfloat16 [128, 512, 1001], P('day', 'pair')
- reference: float32 [512, 1001], P('pair')
All inputs are finite; a program needn't handle non-finite values.
Results may differ from a plain program's by a relative error of at most 0.008.
Values may be sent and summed in bfloat16 or wider, within the bound.
A program may use at most 64 MiB of HBM per device.

v0:
```python
import math

import jax
import jax.numpy as jnp
import numpy as np
from jax import lax
from jax.sharding import PartitionSpec as P

LAGS = 1001
WINDOW = 30


def passed_along(shard, axis, by):
    count = lax.axis_size(axis)
    pairs = [(i, i + by) for i in range(count) if 0 <= i + by < count]
    return lax.ppermute(shard, axis, pairs)


def lag_table(bin_count, lag_count):
    bin_ids = jnp.arange(bin_count, dtype=jnp.int32)[:, None]
    lag_ids = jnp.arange(lag_count, dtype=jnp.int32)[None, :] - (lag_count - 1) // 2
    phase_ids = jnp.mod(bin_ids * lag_ids, 2 * bin_count)
    angle = phase_ids.astype(jnp.float32) * jnp.float32(2.0 * math.pi / (2 * bin_count))
    factor = jnp.float32(1.0 / math.sqrt(2 * bin_count))
    return jnp.concatenate([jnp.cos(angle) * factor, -jnp.sin(angle) * factor], 0).astype(
        jnp.bfloat16
    )


def window_weights(days_here, distance):
    weights = np.zeros((days_here, days_here), np.float32)
    for row_out in range(days_here):
        for row_in in range(days_here):
            offset = row_in - distance * days_here
            if row_out - WINDOW < offset <= row_out:
                weights[row_out, row_in] = 1.0
    return jnp.asarray(weights, dtype=jnp.bfloat16)


def per_device(spectra, pair_stations, availability):
    days_here = spectra.shape[0]
    station_count = spectra.shape[1] * lax.axis_size("pair")
    bin_count = spectra.shape[2] // 2
    inverse = lag_table(bin_count, LAGS)
    station_one = pair_stations[:, 0]
    station_two = pair_stations[:, 1]
    station_ids = jnp.arange(station_count, dtype=jnp.int32)
    pick_one = (station_one[:, None] == station_ids[None, :]).astype(jnp.float32)
    pick_two = (station_two[:, None] == station_ids[None, :]).astype(jnp.float32)
    avail_wide = availability.astype(jnp.float32)
    present = jnp.dot(avail_wide, pick_one.T, precision=lax.Precision.HIGHEST) * jnp.dot(
        avail_wide, pick_two.T, precision=lax.Precision.HIGHEST
    )
    present_half = present.astype(jnp.bfloat16)
    gathered = lax.all_gather(spectra, "pair", axis=1, tiled=True)
    spec_one = jnp.take(gathered, station_one, axis=1)
    spec_two = jnp.take(gathered, station_two, axis=1)
    day_rows = []
    for day_index in range(days_here):
        first_spec = spec_one[day_index].astype(jnp.float32)
        second_spec = spec_two[day_index].astype(jnp.float32)
        real_one, imag_one = (first_spec[:, :bin_count], first_spec[:, bin_count:])
        real_two, imag_two = (second_spec[:, :bin_count], second_spec[:, bin_count:])
        real_part = real_one * real_two + imag_one * imag_two
        imag_part = real_one * imag_two - imag_one * real_two
        cross = jnp.concatenate([real_part, imag_part], 1).astype(jnp.bfloat16)
        corr = jnp.dot(cross, inverse, preferred_element_type=jnp.float32)
        day_rows.append((corr * present[day_index][:, None]).astype(jnp.bfloat16))
    daily = jnp.stack(day_rows, 0)
    total = jnp.sum(daily, axis=0, dtype=jnp.float32)
    day_total = lax.axis_size("day") * days_here
    ref_stack = lax.psum(total, "day") / day_total
    scale = jnp.sqrt(jnp.mean(ref_stack * ref_stack, axis=1) + 1e-06)
    span = (WINDOW + days_here - 2) // days_here
    own_weights = window_weights(days_here, 0)
    moving = jnp.einsum("ij,jpl->ipl", own_weights, daily, preferred_element_type=jnp.float32)
    counts = jnp.einsum("ij,jp->ip", own_weights, present_half, preferred_element_type=jnp.float32)
    for distance in range(1, span + 1):
        far_daily, far_present = passed_along((daily, present_half), "day", distance)
        weights = window_weights(days_here, distance)
        moving = moving + jnp.einsum(
            "ij,jpl->ipl", weights, far_daily, preferred_element_type=jnp.float32
        )
        counts = counts + jnp.einsum(
            "ij,jp->ip", weights, far_present, preferred_element_type=jnp.float32
        )
    stacks = moving / jnp.maximum(counts, 1.0)[:, :, None] / scale[None, :, None]
    return (stacks.astype(jnp.bfloat16), ref_stack)


def solution(mesh):
    return jax.shard_map(
        per_device,
        mesh=mesh,
        in_specs=(P("day", "pair", None), P("pair", None), P("day", None)),
        out_specs=(P("day", "pair", None), P("pair", None)),
        check_vma=False,
    )
```

profile of v0, /device:TPU:2, one launch (start us, length us, event | category | flops | bytes accessed | tf_op | source)
XLA Modules:
  0.0 511.7 jit_solution(7780756500752966899)
XLA Ops:
  9.7 9.0 %collective-permute-start.29 = (bf16[2,64]{1,0:T(2,128)(2,1)S(1)}, bf16[2,64]{1,0:T(2,128)(2,1)S(1)}, u32[]{:S(2)}, u32[]{:S(2)}) collective-permute-start(bf16[2,64]{1,0:T(2,128)(2,1)S(1)} %get-tuple-element.31), channel_id=1, source_target_pairs={{0,120},{8,128},{16,136},{24,144},{32,152},{40,160},{48,168},{56,1... | collective-permute-start | bytes 776 | tf_op jit(solution)/shard_map/ppermute | solution.py:16
  18.7 9.2 %collective-permute-start.28 = (bf16[2,64]{1,0:T(2,128)(2,1)S(1)}, bf16[2,64]{1,0:T(2,128)(2,1)S(1)}, u32[]{:S(2)}, u32[]{:S(2)}) collective-permute-start(bf16[2,64]{1,0:T(2,128)(2,1)S(1)} %get-tuple-element.31), channel_id=1, source_target_pairs={{0,112},{8,120},{16,128},{24,136},{32,144},{40,152},{48,160},{56,1... | collective-permute-start | bytes 776 | tf_op jit(solution)/shard_map/ppermute | solution.py:16
  27.9 6.4 %collective-permute-start.27 = (bf16[2,64]{1,0:T(2,128)(2,1)S(1)}, bf16[2,64]{1,0:T(2,128)(2,1)S(1)}, u32[]{:S(2)}, u32[]{:S(2)}) collective-permute-start(bf16[2,64]{1,0:T(2,128)(2,1)S(1)} %get-tuple-element.31), channel_id=1, source_target_pairs={{0,104},{8,112},{16,120},{24,128},{32,136},{40,144},{48,152},{56,1... | collective-permute-start | bytes 776 | tf_op jit(solution)/shard_map/ppermute | solution.py:16
  34.3 3.8 collective-permute-start.26
  38.1 3.8 collective-permute-start.15
  44.7 35.3 %multiply_convert_fusion.1 = (bf16[2048,1001]{1,0:T(8,128)(2,1)}, bf16[2048,1001]{1,0:T(8,128)(2,1)}) fusion(s32[1001]{0:T(1024)S(1)} %iota_add_fusion), kind=kLoop, calls=%fused_computation.10 | loop fusion | flops 38950912 | bytes 8204196 | tf_op jit(solution)/shard_map/convert.6
  80.2 2.7 collective-permute-start.25
  83.1 4.1 collective-permute-start.24
  90.5 5.1 %collective-permute-start.21 = (bf16[2,64]{1,0:T(2,128)(2,1)S(1)}, bf16[2,64]{1,0:T(2,128)(2,1)S(1)}, u32[]{:S(2)}, u32[]{:S(2)}) collective-permute-start(bf16[2,64]{1,0:T(2,128)(2,1)S(1)} %get-tuple-element.31), channel_id=1, source_target_pairs={{0,56},{8,64},{16,72},{24,80},{32,88},{40,96},{48,104},{56,112},{6... | collective-permute-start | bytes 776 | tf_op jit(solution)/shard_map/ppermute | solution.py:16
  102.7 3.7 collective-permute-start.17
  106.5 3.5 collective-permute-start.16
  111.4 4.2 gather_fusion.1
  117.1 4.2 gather_fusion
  131.6 3.1 collective-permute-start.14
  140.3 3.8 collective-permute-start.10
  147.1 68.5 %collective-permute-start.9 = (bf16[2,64,1001]{2,1,0:T(8,128)(2,1)S(1)}, bf16[2,64,1001]{2,1,0:T(8,128)(2,1)S(1)}, u32[]{:S(2)}, u32[]{:S(2)}) collective-permute-start(bf16[2,64,1001]{2,1,0:T(8,128)(2,1)S(1)} %pad_maximum_fusion.15), channel_id=1, source_target_pairs={{0,80},{8,88},{16,96},{24,104},{32,112},{40,120},{48,128},{56,136}... | collective-permute-start | bytes 768776 | tf_op jit(solution)/shard_map/ppermute | solution.py:16
  217.7 10.0 %collective-permute-start.7 = (bf16[2,64,1001]{2,1,0:T(8,128)(2,1)S(1)}, bf16[2,64,1001]{2,1,0:T(8,128)(2,1)S(1)}, u32[]{:S(2)}, u32[]{:S(2)}) collective-permute-start(bf16[2,64,1001]{2,1,0:T(8,128)(2,1)S(1)} %pad_maximum_fusion.15), channel_id=1, source_target_pairs={{0,64},{8,72},{16,80},{24,88},{32,96},{40,104},{48,112},{56,120},{... | collective-permute-start | bytes 768776 | tf_op jit(solution)/shard_map/ppermute | solution.py:16
  228.2 18.0 %collective-permute-start.6 = (bf16[2,64,1001]{2,1,0:T(8,128)(2,1)S(1)}, bf16[2,64,1001]{2,1,0:T(8,128)(2,1)S(1)}, u32[]{:S(2)}, u32[]{:S(2)}) collective-permute-start(bf16[2,64,1001]{2,1,0:T(8,128)(2,1)S(1)} %pad_maximum_fusion.15), channel_id=1, source_target_pairs={{0,56},{8,64},{16,72},{24,80},{32,88},{40,96},{48,104},{56,112},{6... | collective-permute-start | bytes 768776 | tf_op jit(solution)/shard_map/ppermute | solution.py:16
  249.2 4.4 collective-permute-start.4
  254.9 22.0 %collective-permute-start.3 = (bf16[2,64,1001]{2,1,0:T(8,128)(2,1)S(1)}, bf16[2,64,1001]{2,1,0:T(8,128)(2,1)S(1)}, u32[]{:S(2)}, u32[]{:S(2)}) collective-permute-start(bf16[2,64,1001]{2,1,0:T(8,128)(2,1)S(1)} %pad_maximum_fusion.15), channel_id=1, source_target_pairs={{0,32},{8,40},{16,48},{24,56},{32,64},{40,72},{48,80},{56,88},{64,... | collective-permute-start | bytes 768776 | tf_op jit(solution)/shard_map/ppermute | solution.py:16
  280.7 4.6 collective-permute-start.1
  286.5 4.6 collective-permute-start
  294.8 201.2 %all-reduce.2.cloned.1.call-done = f32[64,1001]{1,0:T(8,128)} async-done(((f32[64,1001]{1,0:T(8,128)}), f32[64,1001]{1,0:T(8,128)}) %all-reduce.2.cloned.1.call-update) | async-done | bytes 256272 | tf_op jit(solution)/shard_map/psum | solution.py:72
  499.8 4.4 fusion.29
  (113 shorter events, 57.3 us)
Async XLA Ops:
  7.2 104.2 %all-gather.2.cloned.1.call-start = ((), (), s32[]{:S(2)}) async-start(), calls=%async_computation | async-start | bytes 2359296 | tf_op jit(solution)/shard_map/all_gather | solution.py:55
  9.7 73.3 %collective-permute-start.29 = (bf16[2,64]{1,0:T(2,128)(2,1)S(1)}, bf16[2,64]{1,0:T(2,128)(2,1)S(1)}, u32[]{:S(2)}, u32[]{:S(2)}) collective-permute-start(bf16[2,64]{1,0:T(2,128)(2,1)S(1)} %get-tuple-element.31), channel_id=1, source_target_pairs={{0,120},{8,128},{16,136},{24,144},{32,152},{40,160},{48,168},{56,1... | collective-permute-start | bytes 776 | tf_op jit(solution)/shard_map/ppermute | solution.py:16
  18.7 68.5 %collective-permute-start.28 = (bf16[2,64]{1,0:T(2,128)(2,1)S(1)}, bf16[2,64]{1,0:T(2,128)(2,1)S(1)}, u32[]{:S(2)}, u32[]{:S(2)}) collective-permute-start(bf16[2,64]{1,0:T(2,128)(2,1)S(1)} %get-tuple-element.31), channel_id=1, source_target_pairs={{0,112},{8,120},{16,128},{24,136},{32,144},{40,152},{48,160},{56,1... | collective-permute-start | bytes 776 | tf_op jit(solution)/shard_map/ppermute | solution.py:16
  27.9 61.0 %collective-permute-start.27 = (bf16[2,64]{1,0:T(2,128)(2,1)S(1)}, bf16[2,64]{1,0:T(2,128)(2,1)S(1)}, u32[]{:S(2)}, u32[]{:S(2)}) collective-permute-start(bf16[2,64]{1,0:T(2,128)(2,1)S(1)} %get-tuple-element.31), channel_id=1, source_target_pairs={{0,104},{8,112},{16,120},{24,128},{32,136},{40,144},{48,152},{56,1... | collective-permute-start | bytes 776 | tf_op jit(solution)/shard_map/ppermute | solution.py:16
  34.3 56.2 %collective-permute-start.26 = (bf16[2,64]{1,0:T(2,128)(2,1)S(1)}, bf16[2,64]{1,0:T(2,128)(2,1)S(1)}, u32[]{:S(2)}, u32[]{:S(2)}) collective-permute-start(bf16[2,64]{1,0:T(2,128)(2,1)S(1)} %get-tuple-element.31), channel_id=1, source_target_pairs={{0,96},{8,104},{16,112},{24,120},{32,128},{40,136},{48,144},{56,15... | collective-permute-start | bytes 776 | tf_op jit(solution)/shard_map/ppermute | solution.py:16
  38.1 42.1 %collective-permute-start.15 = (bf16[2,64]{1,0:T(2,128)(2,1)S(1)}, bf16[2,64]{1,0:T(2,128)(2,1)S(1)}, u32[]{:S(2)}, u32[]{:S(2)}) collective-permute-start(bf16[2,64]{1,0:T(2,128)(2,1)S(1)} %get-tuple-element.31), channel_id=1, source_target_pairs={{0,8},{8,16},{16,24},{24,32},{32,40},{40,48},{48,56},{56,64},{64,7... | collective-permute-start | bytes 776 | tf_op jit(solution)/shard_map/ppermute | solution.py:16
  43.9 452.1 %all-reduce.2.cloned.1.call-start = ((), (), s32[]{:S(2)}) async-start(), calls=%async_computation.1 | async-start | bytes 524288 | tf_op jit(solution)/shard_map/psum | solution.py:72
  80.2 15.5 %collective-permute-start.25 = (bf16[2,64]{1,0:T(2,128)(2,1)S(1)}, bf16[2,64]{1,0:T(2,128)(2,1)S(1)}, u32[]{:S(2)}, u32[]{:S(2)}) collective-permute-start(bf16[2,64]{1,0:T(2,128)(2,1)S(1)} %get-tuple-element.31), channel_id=1, source_target_pairs={{0,88},{8,96},{16,104},{24,112},{32,120},{40,128},{48,136},{56,144... | collective-permute-start | bytes 776 | tf_op jit(solution)/shard_map/ppermute | solution.py:16
  83.1 14.6 %collective-permute-start.24 = (bf16[2,64]{1,0:T(2,128)(2,1)S(1)}, bf16[2,64]{1,0:T(2,128)(2,1)S(1)}, u32[]{:S(2)}, u32[]{:S(2)}) collective-permute-start(bf16[2,64]{1,0:T(2,128)(2,1)S(1)} %get-tuple-element.31), channel_id=1, source_target_pairs={{0,80},{8,88},{16,96},{24,104},{32,112},{40,120},{48,128},{56,136}... | collective-permute-start | bytes 776 | tf_op jit(solution)/shard_map/ppermute | solution.py:16
  90.5 16.0 %collective-permute-start.21 = (bf16[2,64]{1,0:T(2,128)(2,1)S(1)}, bf16[2,64]{1,0:T(2,128)(2,1)S(1)}, u32[]{:S(2)}, u32[]{:S(2)}) collective-permute-start(bf16[2,64]{1,0:T(2,128)(2,1)S(1)} %get-tuple-element.31), channel_id=1, source_target_pairs={{0,56},{8,64},{16,72},{24,80},{32,88},{40,96},{48,104},{56,112},{6... | collective-permute-start | bytes 776 | tf_op jit(solution)/shard_map/ppermute | solution.py:16
  131.6 366.2 %collective-permute-start.14 = (bf16[2,64,1001]{2,1,0:T(8,128)(2,1)S(1)}, bf16[2,64,1001]{2,1,0:T(8,128)(2,1)S(1)}, u32[]{:S(2)}, u32[]{:S(2)}) collective-permute-start(bf16[2,64,1001]{2,1,0:T(8,128)(2,1)S(1)} %pad_maximum_fusion.15), channel_id=1, source_target_pairs={{0,120},{8,128},{16,136},{24,144},{32,152},{40,160},{48,168},{56,1... | collective-permute-start | bytes 768776 | tf_op jit(solution)/shard_map/ppermute | solution.py:16
  136.6 79.4 %collective-permute-start.12 = (bf16[2,64,1001]{2,1,0:T(8,128)(2,1)S(1)}, bf16[2,64,1001]{2,1,0:T(8,128)(2,1)S(1)}, u32[]{:S(2)}, u32[]{:S(2)}) collective-permute-start(bf16[2,64,1001]{2,1,0:T(8,128)(2,1)S(1)} %pad_maximum_fusion.15), channel_id=1, source_target_pairs={{0,104},{8,112},{16,120},{24,128},{32,136},{40,144},{48,152},{56,1... | collective-permute-start | bytes 768776 | tf_op jit(solution)/shard_map/ppermute | solution.py:16
  138.2 79.5 %collective-permute-start.11 = (bf16[2,64,1001]{2,1,0:T(8,128)(2,1)S(1)}, bf16[2,64,1001]{2,1,0:T(8,128)(2,1)S(1)}, u32[]{:S(2)}, u32[]{:S(2)}) collective-permute-start(bf16[2,64,1001]{2,1,0:T(8,128)(2,1)S(1)} %pad_maximum_fusion.15), channel_id=1, source_target_pairs={{0,96},{8,104},{16,112},{24,120},{32,128},{40,136},{48,144},{56,15... | collective-permute-start | bytes 768776 | tf_op jit(solution)/shard_map/ppermute | solution.py:16
  140.3 87.9 %collective-permute-start.10 = (bf16[2,64,1001]{2,1,0:T(8,128)(2,1)S(1)}, bf16[2,64,1001]{2,1,0:T(8,128)(2,1)S(1)}, u32[]{:S(2)}, u32[]{:S(2)}) collective-permute-start(bf16[2,64,1001]{2,1,0:T(8,128)(2,1)S(1)} %pad_maximum_fusion.15), channel_id=1, source_target_pairs={{0,88},{8,96},{16,104},{24,112},{32,120},{40,128},{48,136},{56,144... | collective-permute-start | bytes 768776 | tf_op jit(solution)/shard_map/ppermute | solution.py:16
  147.1 99.6 %collective-permute-start.9 = (bf16[2,64,1001]{2,1,0:T(8,128)(2,1)S(1)}, bf16[2,64,1001]{2,1,0:T(8,128)(2,1)S(1)}, u32[]{:S(2)}, u32[]{:S(2)}) collective-permute-start(bf16[2,64,1001]{2,1,0:T(8,128)(2,1)S(1)} %pad_maximum_fusion.15), channel_id=1, source_target_pairs={{0,80},{8,88},{16,96},{24,104},{32,112},{40,120},{48,128},{56,136}... | collective-permute-start | bytes 768776 | tf_op jit(solution)/shard_map/ppermute | solution.py:16
  216.0 33.3 %collective-permute-start.8 = (bf16[2,64,1001]{2,1,0:T(8,128)(2,1)S(1)}, bf16[2,64,1001]{2,1,0:T(8,128)(2,1)S(1)}, u32[]{:S(2)}, u32[]{:S(2)}) collective-permute-start(bf16[2,64,1001]{2,1,0:T(8,128)(2,1)S(1)} %pad_maximum_fusion.15), channel_id=1, source_target_pairs={{0,72},{8,80},{16,88},{24,96},{32,104},{40,112},{48,120},{56,128},... | collective-permute-start | bytes 768776 | tf_op jit(solution)/shard_map/ppermute | solution.py:16
  217.7 37.2 %collective-permute-start.7 = (bf16[2,64,1001]{2,1,0:T(8,128)(2,1)S(1)}, bf16[2,64,1001]{2,1,0:T(8,128)(2,1)S(1)}, u32[]{:S(2)}, u32[]{:S(2)}) collective-permute-start(bf16[2,64,1001]{2,1,0:T(8,128)(2,1)S(1)} %pad_maximum_fusion.15), channel_id=1, source_target_pairs={{0,64},{8,72},{16,80},{24,88},{32,96},{40,104},{48,112},{56,120},{... | collective-permute-start | bytes 768776 | tf_op jit(solution)/shard_map/ppermute | solution.py:16
  228.2 50.0 %collective-permute-start.6 = (bf16[2,64,1001]{2,1,0:T(8,128)(2,1)S(1)}, bf16[2,64,1001]{2,1,0:T(8,128)(2,1)S(1)}, u32[]{:S(2)}, u32[]{:S(2)}) collective-permute-start(bf16[2,64,1001]{2,1,0:T(8,128)(2,1)S(1)} %pad_maximum_fusion.15), channel_id=1, source_target_pairs={{0,56},{8,64},{16,72},{24,80},{32,88},{40,96},{48,104},{56,112},{6... | collective-permute-start | bytes 768776 | tf_op jit(solution)/shard_map/ppermute | solution.py:16
  246.7 34.0 %collective-permute-start.5 = (bf16[2,64,1001]{2,1,0:T(8,128)(2,1)S(1)}, bf16[2,64,1001]{2,1,0:T(8,128)(2,1)S(1)}, u32[]{:S(2)}, u32[]{:S(2)}) collective-permute-start(bf16[2,64,1001]{2,1,0:T(8,128)(2,1)S(1)} %pad_maximum_fusion.15), channel_id=1, source_target_pairs={{0,48},{8,56},{16,64},{24,72},{32,80},{40,88},{48,96},{56,104},{64... | collective-permute-start | bytes 768776 | tf_op jit(solution)/shard_map/ppermute | solution.py:16
  249.2 37.3 %collective-permute-start.4 = (bf16[2,64,1001]{2,1,0:T(8,128)(2,1)S(1)}, bf16[2,64,1001]{2,1,0:T(8,128)(2,1)S(1)}, u32[]{:S(2)}, u32[]{:S(2)}) collective-permute-start(bf16[2,64,1001]{2,1,0:T(8,128)(2,1)S(1)} %pad_maximum_fusion.15), channel_id=1, source_target_pairs={{0,40},{8,48},{16,56},{24,64},{32,72},{40,80},{48,88},{56,96},{64,... | collective-permute-start | bytes 768776 | tf_op jit(solution)/shard_map/ppermute | solution.py:16
  254.9 37.5 %collective-permute-start.3 = (bf16[2,64,1001]{2,1,0:T(8,128)(2,1)S(1)}, bf16[2,64,1001]{2,1,0:T(8,128)(2,1)S(1)}, u32[]{:S(2)}, u32[]{:S(2)}) collective-permute-start(bf16[2,64,1001]{2,1,0:T(8,128)(2,1)S(1)} %pad_maximum_fusion.15), channel_id=1, source_target_pairs={{0,32},{8,40},{16,48},{24,56},{32,64},{40,72},{48,80},{56,88},{64,... | collective-permute-start | bytes 768776 | tf_op jit(solution)/shard_map/ppermute | solution.py:16
  278.2 15.4 %collective-permute-start.2 = (bf16[2,64,1001]{2,1,0:T(8,128)(2,1)S(1)}, bf16[2,64,1001]{2,1,0:T(8,128)(2,1)S(1)}, u32[]{:S(2)}, u32[]{:S(2)}) collective-permute-start(bf16[2,64,1001]{2,1,0:T(8,128)(2,1)S(1)} %pad_maximum_fusion.15), channel_id=1, source_target_pairs={{0,24},{8,32},{16,40},{24,48},{32,56},{40,64},{48,72},{56,80},{64,... | collective-permute-start | bytes 768776 | tf_op jit(solution)/shard_map/ppermute | solution.py:16
  280.7 219.0 %collective-permute-start.1 = (bf16[2,64,1001]{2,1,0:T(8,128)(2,1)S(1)}, bf16[2,64,1001]{2,1,0:T(8,128)(2,1)S(1)}, u32[]{:S(2)}, u32[]{:S(2)}) collective-permute-start(bf16[2,64,1001]{2,1,0:T(8,128)(2,1)S(1)} %pad_maximum_fusion.15), channel_id=1, source_target_pairs={{0,16},{8,24},{16,32},{24,40},{32,48},{40,56},{48,64},{56,72},{64,... | collective-permute-start | bytes 768776 | tf_op jit(solution)/shard_map/ppermute | solution.py:16
  286.5 211.7 %collective-permute-start = (bf16[2,64,1001]{2,1,0:T(8,128)(2,1)S(1)}, bf16[2,64,1001]{2,1,0:T(8,128)(2,1)S(1)}, u32[]{:S(2)}, u32[]{:S(2)}) collective-permute-start(bf16[2,64,1001]{2,1,0:T(8,128)(2,1)S(1)} %pad_maximum_fusion.15), channel_id=1, source_target_pairs={{0,8},{8,16},{16,24},{24,32},{32,40},{40,48},{48,56},{56,64},{64,7... | collective-permute-start | bytes 768776 | tf_op jit(solution)/shard_map/ppermute | solution.py:16
  (14 other events, 437.9 us)
Sparse Core Ops, SparseCore 0:
  44.0 22.6 all-gather.1
  145.0 350.9 all-reduce.1
where the time goes:
time: 513 us; the launch traced here: 512 us
  starting transfers between devices  210 us (41%)
  waiting for transfers between devices  203 us (40%)
  other arithmetic  44.5 us (9%)
  matrix products  25.7 us (5%)
  local copies, waits for them, and re-layouts  14.7 us (3%)
  between operations  14.6 us (3%)
    ppermute x30, starting transfers between devices, passed_along(): return lax.ppermute(shard, axis, pairs)  209 us
    psum x1, waiting for transfers between devices, per_device(): ref_stack = lax.psum(total, 'day') / day_total  201 us
    another operation x3, other arithmetic  35.7 us
    dot_general x15, matrix products, per_device(): jnp.einsum('ij,jpl->ipl', weights, far_daily, preferred_element_type=jnp....  17.7 us
  transfers between devices with their start and end apart: 32, of which 3 were waited for; matrix products, arithmetic and copies ran while one was open for 11% of the time, Pallas kernels for 0%

commit v1 on v0

v1 whole, which is shorter than its diff:
```python
import jax
import jax.numpy as jnp
import numpy as np
from jax import lax
from jax.sharding import PartitionSpec as P

LAGS = 1001
WIDE = 1024
WINDOW = 30


def lag_table(bin_count):
    bin_ids = np.arange(bin_count)[:, None]
    lag_ids = np.arange(LAGS)[None, :] - (LAGS - 1) // 2
    angle = np.mod(bin_ids * lag_ids, 2 * bin_count) * (np.pi / bin_count)
    factor = 1.0 / np.sqrt(2.0 * bin_count)
    table = np.concatenate([np.cos(angle) * factor, -np.sin(angle) * factor], 0)
    return np.pad(table, ((0, 0), (0, WIDE - LAGS))).astype(np.float32).astype(jnp.bfloat16)


def per_device(spectra, pair_stations, availability):
    days_here = spectra.shape[0]
    groups = lax.axis_size("day")
    station_count = spectra.shape[1] * lax.axis_size("pair")
    bin_count = spectra.shape[2] // 2
    pairs_here = pair_stations.shape[0]
    inverse = jnp.asarray(lag_table(bin_count))
    station_ids = jnp.arange(station_count, dtype=jnp.int32)
    ends = jnp.concatenate([pair_stations[:, 0], pair_stations[:, 1]], 0)
    pick = (ends[:, None] == station_ids[None, :]).astype(jnp.bfloat16)
    avail = jnp.dot(availability.astype(jnp.bfloat16), pick.T, preferred_element_type=jnp.float32)
    present = avail[:, :pairs_here] * avail[:, pairs_here:]
    gathered = lax.all_gather(spectra, "pair", axis=1, tiled=True)
    rows = []
    for day in range(days_here):
        spec = jnp.dot(pick, gathered[day], preferred_element_type=jnp.float32)
        one, two = spec[:pairs_here], spec[pairs_here:]
        ar, ai, br, bi = one[:, :bin_count], one[:, bin_count:], two[:, :bin_count], two[:, bin_count:]
        rows.append(jnp.concatenate([ar * br + ai * bi, ar * bi - ai * br], 1).astype(jnp.bfloat16))
    cross = jnp.concatenate(rows, 0)
    corr = jnp.dot(cross, inverse, preferred_element_type=jnp.float32)
    column = lax.broadcasted_iota(jnp.int32, (1, WIDE), 1)
    shown = present.reshape(-1, 1)
    daily = jnp.where(column == LAGS, shown, corr * shown).astype(jnp.bfloat16)
    daily = daily.reshape(days_here, pairs_here, WIDE)
    turned = lax.all_to_all(daily, "day", split_axis=1, concat_axis=0, tiled=True)
    days = groups * days_here
    mine = turned.reshape(days, WIDE)
    day_ids = np.arange(days)
    gap = day_ids[:, None] - day_ids[None, :]
    band = jnp.asarray(((gap >= 0) & (gap < WINDOW)).astype(np.float32), dtype=jnp.bfloat16)
    moving = jnp.dot(band, mine, preferred_element_type=jnp.float32)
    counts = moving[:, LAGS:LAGS + 1]
    ref = jnp.sum(mine.astype(jnp.float32), axis=0) / days
    ref = jnp.where(column[0] < LAGS, ref, 0.0)
    scale = jnp.sqrt(jnp.sum(ref * ref) / LAGS + 1e-06)
    stacks = (moving / jnp.maximum(counts, 1.0) / scale).astype(jnp.bfloat16)
    back = lax.all_to_all(stacks.reshape(days, 1, WIDE), "day", split_axis=0, concat_axis=1, tiled=True)
    ref_all = lax.all_gather(ref[None], "day", axis=0, tiled=True)
    return back[:, :, :LAGS], ref_all[:, :LAGS]


def solution(mesh):
    return jax.shard_map(
        per_device,
        mesh=mesh,
        in_specs=(P("day", "pair", None), P("pair", None), P("day", None)),
        out_specs=(P("day", "pair", None), P("pair", None)),
        check_vma=False,
    )
```

time: 513 us -> 199 us (0.39)
  the two profiles are of different devices: /device:TPU:2 before, /device:TPU:8 now
where the time goes in v1:
time: 199 us
  blocking collectives  124 us (62%)
  waiting for transfers between devices  38.3 us (19%)
  between operations  14.8 us (7%)
  local copies, waits for them, and re-layouts  6.83 us (3%)
  starting transfers between devices  5.97 us (3%)
  matrix products  4.73 us (2%)
  other arithmetic  4.04 us (2%)
    all_gather x1, blocking collectives, per_device(): ref_all = lax.all_gather(ref[None], 'day', axis=0, tiled=True)  86.4 us
    all_gather x1, waiting for transfers between devices, per_device(): gathered = lax.all_gather(spectra, 'pair', axis=1, tiled=True)  37.6 us
    all_to_all x1, blocking collectives, per_device(): lax.all_to_all(daily, 'day', split_axis=1, concat_axis=0, tiled=True)  37.4 us
    all_to_all x1, starting transfers between devices, per_device(): lax.all_to_all(stacks.reshape(days, 1, WIDE), 'day', split_axis=0, concat...  5.93 us
    unnamed x10, local copies, waits for them, and re-layouts  5.05 us
  transfers between devices with their start and end apart: 2, of which 1 were waited for; matrix products, arithmetic and copies ran while one was open for 1% of the time, Pallas kernels for 0%

profile of v1, /device:TPU:8, one launch (start us, length us, event | category | flops | bytes accessed | tf_op | source)
XLA Modules:
  0.0 198.5 jit_solution(13838983268094882941)
XLA Ops:
  7.2 0.7 all-gather.3.cloned.1.call-update
  7.9 0.8 slice_bitcast_fusion.5
  8.7 0.9 convolution_bitcast_fusion
  9.8 37.6 %all-gather.3.cloned.1.call-done = bf16[2,128,4096]{2,1,0:T(8,128)(2,1)} async-done(((bf16[2,16,4096]{2,1,0:T(8,128)(2,1)}), bf16[2,128,4096]{2,1,0:T(8,128)(2,1)}) %all-gather.3.cloned.1.call-update) | async-done | bytes 2097168 | tf_op jit(solution)/shard_map/all_gather | solution.py:33
  47.4 1.8 fusion.3
  49.3 0.5 fusion.2
  49.8 0.4 add_convert_fusion
  50.2 2.5 %copy-done.2 = bf16[4096,1024]{1,0:T(8,128)(2,1)S(1)} copy-done((bf16[4096,1024]{1,0:T(8,128)(2,1)S(1)}, bf16[4096,1024]{1,0:T(8,128)(2,1)}, u32[]{:S(2)}) %copy-start.2) | copy-done | bytes 8388632
  52.7 1.3 fusion.1
  54.0 0.3 copy.12
  54.3 37.4 %all_to_all.33 = bf16[2,64,1024]{2,0,1:T(2,128)(2,1)S(1)} all-to-all(bf16[2,64,1024]{2,0,1:T(2,128)(2,1)S(1)} %copy.12), channel_id=1, replica_groups=mesh['day'=64,'pair'=8] {'day'}, dimensions={1} | all-to-all | bytes 524288 | tf_op jit(solution)/shard_map/all_to_all | solution.py:46
  91.7 0.2 convert_reduce_fusion
  91.9 0.6 broadcast_multiply_fusion
  93.3 0.2 fusion.18
  93.5 0.2 fusion.11
  93.8 0.5 broadcast.36
  94.3 0.8 reduce.6
  95.1 0.8 reshape.58
  95.9 5.9 %all-to-all-start.1 = ((bf16[64,2,1024]{2,1,0:T(2,128)(2,1)}), bf16[64,2,1024]{2,1,0:T(2,128)(2,1)S(1)}, u32[]{:S(2)}, u32[]{:S(2)}) async-start(bf16[64,2,1024]{2,1,0:T(2,128)(2,1)} %reshape.58), calls=%async_computation.1 | async-start | bytes 524288 | tf_op jit(solution)/shard_map/all_to_all | solution.py:58
  101.9 86.4 %all-gather = f32[64,1,1024]{2,1,0:T(1,128)S(1)} all-gather(f32[1,1,1024]{2,1,0:T(1,128)S(1)} %fusion.15), channel_id=1, replica_groups=mesh['day'=64,'pair'=8] {'day'}, dimensions={0}, use_global_device_ids=true | all-gather | bytes 266240 | tf_op jit(solution)/shard_map/all_gather | solution.py:59
  188.3 0.8 copy.19
  189.1 0.2 reshape.59
  189.3 1.5 reduce.4
  190.9 0.8 copy.15
  (15 shorter events, 0.6 us)
Async XLA Ops:
  7.2 40.2 %all-gather.3.cloned.1.call-start = ((), (), s32[]{:S(2)}) async-start(), calls=%async_computation.2 | async-start | bytes 2359296 | tf_op jit(solution)/shard_map/all_gather | solution.py:33
  47.4 1.9 copy-start
  49.3 3.4 %copy-start.2 = (bf16[4096,1024]{1,0:T(8,128)(2,1)S(1)}, bf16[4096,1024]{1,0:T(8,128)(2,1)}, u32[]{:S(2)}) copy-start(bf16[4096,1024]{1,0:T(8,128)(2,1)} %constant.19.clone) | copy-start | bytes 25165828
  52.7 40.6 %copy-start.1 = (bf16[128,128]{1,0:T(8,128)(2,1)S(1)}, bf16[128,128]{1,0:T(8,128)(2,1)}, u32[]{:S(2)}) copy-start(bf16[128,128]{1,0:T(8,128)(2,1)} %constant.25) | copy-start | bytes 98308
  95.9 93.1 %all-to-all-start.1 = ((bf16[64,2,1024]{2,1,0:T(2,128)(2,1)}), bf16[64,2,1024]{2,1,0:T(2,128)(2,1)S(1)}, u32[]{:S(2)}, u32[]{:S(2)}) async-start(bf16[64,2,1024]{2,1,0:T(2,128)(2,1)} %reshape.58), calls=%async_computation.1 | async-start | bytes 524288 | tf_op jit(solution)/shard_map/all_to_all | solution.py:58
Sparse Core Ops, SparseCore 0:
  10.1 37.1 all-gather.2

commit v2 on v1

v2 whole, which is shorter than its diff:
```python
import functools

import jax
import jax.numpy as jnp
import numpy as np
from jax import lax
from jax.experimental import pallas as pl
from jax.experimental.pallas import tpu as pltpu
from jax.sharding import PartitionSpec as P

LAGS = 1001
WIDE = 1024
TILES = WIDE // 128
WINDOW = 30
ALONG_X = 4
ALONG_Y = 4
BLOCK = 16
PAD = 16
F32 = jnp.float32
BF16 = jnp.bfloat16


def lag_table(bin_count):
    bin_ids = np.arange(bin_count)[:, None]
    lag_ids = np.arange(LAGS)[None, :] - (LAGS - 1) // 2
    angle = np.mod(bin_ids * lag_ids, 2 * bin_count) * (np.pi / bin_count)
    factor = 1.0 / np.sqrt(2.0 * bin_count)
    table = np.concatenate([np.cos(angle) * factor, -np.sin(angle) * factor], 0)
    return np.pad(table, ((0, 0), (0, WIDE - LAGS))).astype(np.float32).astype(jnp.bfloat16)


def rows(index, count=BLOCK):
    return pl.ds(pl.multiple_of(index * count, count), count)


def kernel(groups, days, spectra, ends, availability, table_hbm, stacks, reference,
           gathered, table, cross, spread, daily, turned, held, ready, back, refs,
           odd_pad, sum_pad, two_pad, four_pad, eight_pad,
           table_sem, own_sem, give, take, day_sems):
    me = lax.axis_index("day")
    mine = lax.axis_index("pair")
    x, core = mine // 2, mine % 2
    z, y = me // ALONG_Y, me % ALONG_Y
    planes = groups // ALONG_Y
    right = ((x + 1) % ALONG_X) * 2 + core
    left = ((x + ALONG_X - 1) % ALONG_X) * 2 + core
    across = ((x + 2) % ALONG_X) * 2 + core
    sibling = x * 2 + 1 - core
    bins2 = spectra.shape[2]
    half = bins2 // 2

    barrier = pltpu.get_barrier_semaphore()
    for other in (right, left, sibling):
        pl.semaphore_signal(barrier, inc=1, device_id={"pair": other}, device_id_type=pl.DeviceIdType.MESH)

    def greet(i, carry):
        pl.semaphore_signal(barrier, inc=1, device_id={"day": (me + i) % groups}, device_id_type=pl.DeviceIdType.MESH)
        return carry

    lax.fori_loop(1, groups, greet, 0)
    table_copy = pltpu.make_async_copy(table_hbm, table, table_sem)
    table_copy.start()
    own_copy = pltpu.make_async_copy(spectra, gathered.at[:, rows(mine)], own_sem)
    own_copy.start()
    pl.semaphore_wait(barrier, groups + 2)

    def to(kind, day, src, dst, other):
        copy = pltpu.make_async_remote_copy(
            src_ref=src, dst_ref=dst, send_sem=give.at[kind, day], recv_sem=take.at[kind, day],
            device_id={"pair": other}, device_id_type=pl.DeviceIdType.MESH)
        copy.start()
        return copy

    first = []
    for day in range(2):
        place = gathered.at[day, rows(mine)]
        first.append((to(0, day, spectra.at[day], place, right),
                      to(1, day, spectra.at[day], place, left),
                      to(2, day, spectra.at[day], place, sibling)))

    for pad in (odd_pad, sum_pad, two_pad, four_pad, eight_pad):
        pad[0:PAD] = jnp.zeros((PAD, 8, 128), F32)
    pairs = ends.shape[1]
    station = lax.broadcasted_iota(jnp.int32, (128, pairs), 0)
    pick_one = jnp.where(station == ends[0:1, :], 1.0, 0.0).astype(F32).T
    pick_two = jnp.where(station == ends[1:2, :], 1.0, 0.0).astype(F32).T
    pick = jnp.concatenate([pick_one, pick_two], 0).astype(BF16)
    shown = []
    for day in range(2):
        there = availability[day:day + 1, :].astype(F32)
        shown.append(jnp.sum(pick_one * there, axis=1, keepdims=True) * jnp.sum(pick_two * there, axis=1, keepdims=True))

    second, third = [], []
    for day in range(2):
        from_left, from_right, from_sibling = first[day]
        part = gathered.at[day, rows(left)]
        from_left.wait_recv()
        ahead = to(3, day, part.at[:, 0:half], part.at[:, 0:half], right)
        down = to(4, day, part, part, sibling)
        part = gathered.at[day, rows(right)]
        from_right.wait_recv()
        second.append((ahead, to(5, day, part.at[:, half:], part.at[:, half:], left), down, to(6, day, part, part, sibling)))
    own_copy.wait()
    for day in range(2):
        from_left, from_right, down_one, down_two = second[day]
        part = gathered.at[day, rows(across)]
        from_left.wait_recv()
        one = to(7, day, part.at[:, 0:half], part.at[:, 0:half], sibling)
        from_right.wait_recv()
        two = to(8, day, part.at[:, half:], part.at[:, half:], sibling)
        third.append((one, two))
        for copy in (first[day][2], down_one, down_two, one, two):
            copy.wait_recv()
        width = min(512, half)
        for at in range(0, half, width):
            real = jnp.dot(pick, gathered[day, :, at:at + width], preferred_element_type=F32)
            imag = jnp.dot(pick, gathered[day, :, half + at:half + at + width], preferred_element_type=F32)
            ar, br, ai, bi = real[:pairs], real[pairs:], imag[:pairs], imag[pairs:]
            cross[day * pairs:(day + 1) * pairs, at:at + width] = (ar * br + ai * bi).astype(BF16)
            cross[day * pairs:(day + 1) * pairs, half + at:half + at + width] = (ar * bi - ai * br).astype(BF16)
    table_copy.wait()
    spare = lax.broadcasted_iota(jnp.int32, (pairs, 128), 1) == LAGS - 128 * (TILES - 1)
    for at in range(0, WIDE, 256):
        corr = jnp.dot(cross[...], table[:, at:at + 256], preferred_element_type=F32)
        for day in range(2):
            for j in range(2):
                tile = at // 128 + j
                part = corr[day * pairs:(day + 1) * pairs, 128 * j:128 * (j + 1)] * shown[day]
                if tile == TILES - 1:
                    part = jnp.where(spare, shown[day], part)
                spread[pl.ds(8 * day + tile, pairs, stride=BLOCK), :] = part
    daily[...] = spread[...].astype(BF16)

    def turn(src, dst, send_sem, recv_sem):
        def copy(to_group):
            return pltpu.make_async_remote_copy(
                src_ref=src.at[rows(to_group)], dst_ref=dst.at[rows(me)], send_sem=send_sem, recv_sem=recv_sem,
                device_id={"day": to_group}, device_id_type=pl.DeviceIdType.MESH)

        def step(i, carry):
            copy((me + i) % groups).start()
            copy((me + groups - i) % groups).start()
            return carry

        lax.fori_loop(1, groups // 2, step, 0)
        copy((me + groups // 2) % groups).start()
        count = (groups - 1) * BLOCK
        return pltpu.make_async_remote_copy(
            src_ref=src.at[0:count], dst_ref=dst.at[0:count], send_sem=send_sem, recv_sem=recv_sem,
            device_id={"day": (me + 1) % groups}, device_id_type=pl.DeviceIdType.MESH)

    there = turn(daily, turned, day_sems.at[0], day_sems.at[1])
    turned[rows(me), :] = daily[rows(me), :]
    there.wait_recv()

    blocks = turned[...].astype(F32).reshape(groups, BLOCK, 128)
    even, odd = blocks[:, :8], blocks[:, 8:]
    both = even + odd
    own = slice(PAD, PAD + groups)

    def past(ref, by):
        return ref[PAD - by:PAD - by + groups]

    odd_pad[own] = odd
    sum_pad[own] = both
    two = both + past(sum_pad, 1)
    two_pad[own] = two
    four = two + past(two_pad, 2)
    four_pad[own] = four
    eight_pad[own] = four + past(four_pad, 4)
    full = past(eight_pad, 1) + past(four_pad, 9) + past(two_pad, 13)
    ref_row = jnp.sum(both, axis=0) / days
    lag = 128 * lax.broadcasted_iota(jnp.int32, (8, 128), 0) + lax.broadcasted_iota(jnp.int32, (8, 128), 1)
    power = jnp.sum(jnp.where(lag < LAGS, ref_row * ref_row, 0.0), axis=(0, 1), keepdims=True) / LAGS
    scale = jnp.sqrt(power + 1e-06)[None]
    refs[z, rows(y, 8), :] = ref_row

    def along_z(plane):
        return pltpu.make_async_remote_copy(
            src_ref=refs.at[z, rows(y, 8)], dst_ref=refs.at[z, rows(y, 8)], send_sem=day_sems.at[4], recv_sem=day_sems.at[5],
            device_id={"day": plane * ALONG_Y + y}, device_id_type=pl.DeviceIdType.MESH)

    def step_z(i, carry):
        along_z((z + i) % planes).start()
        return carry

    lax.fori_loop(1, planes, step_z, 0)
    spot = LAGS - 128 * (TILES - 1)

    def normalised(moving):
        counts = moving[:, 7:8, spot:spot + 1]
        return moving * (1.0 / (jnp.maximum(counts, 1.0) * scale))

    ready[...] = jnp.concatenate(
        [normalised(full + past(odd_pad, 15) + even), normalised(full + both)], 1).reshape(groups * BLOCK, 128).astype(BF16)
    home = turn(ready, back, day_sems.at[2], day_sems.at[3])
    back[rows(me), :] = ready[rows(me), :]

    got_z = pltpu.make_async_remote_copy(
        src_ref=refs.at[0:planes - 1, 0:8], dst_ref=refs.at[0:planes - 1, 0:8], send_sem=day_sems.at[4], recv_sem=day_sems.at[5],
        device_id={"day": ((z + 1) % planes) * ALONG_Y + y}, device_id_type=pl.DeviceIdType.MESH)
    got_z.wait_recv()
    for i in range(1, ALONG_Y):
        pltpu.make_async_remote_copy(
            src_ref=refs.at[:, rows(y, 8)], dst_ref=refs.at[:, rows(y, 8)], send_sem=day_sems.at[6], recv_sem=day_sems.at[7],
            device_id={"day": z * ALONG_Y + (y + i) % ALONG_Y}, device_id_type=pl.DeviceIdType.MESH).start()
    got_y = pltpu.make_async_remote_copy(
        src_ref=refs.at[:, 0:24], dst_ref=refs.at[:, 0:24], send_sem=day_sems.at[6], recv_sem=day_sems.at[7],
        device_id={"day": z * ALONG_Y + (y + 1) % ALONG_Y}, device_id_type=pl.DeviceIdType.MESH)
    got_y.wait_recv()
    held[...] = refs[...].reshape(groups * 8, 128)
    for tile in range(TILES):
        wide = min(128, LAGS - 128 * tile)
        reference[:, 128 * tile:128 * tile + wide] = held[pl.ds(tile, groups, stride=8), :][:, :wide]

    home.wait_recv()
    spread[...] = back[...].astype(F32)
    for day in range(2):
        for tile in range(TILES):
            wide = min(128, LAGS - 128 * tile)
            part = spread[pl.ds(8 * day + tile, groups, stride=BLOCK), :].astype(BF16)
            stacks[day, :, 128 * tile:128 * tile + wide] = part[:, :wide]

    for day in range(2):
        for copy in first[day] + second[day] + third[day]:
            copy.wait_send()
    there.wait_send()
    home.wait_send()
    got_z.wait_send()
    got_y.wait_send()


def per_device(spectra, pair_stations, availability):
    groups = lax.axis_size("day")
    days_here, shard, bins2 = spectra.shape
    stations = shard * lax.axis_size("pair")
    pairs = pair_stations.shape[0]
    table = jnp.asarray(lag_table(bins2 // 2))
    vmem = pl.BlockSpec(memory_space=pltpu.VMEM)
    anywhere = pl.BlockSpec(memory_space=pl.ANY)
    padded = pltpu.VMEM((PAD + groups, 8, 128), F32)
    block = pltpu.VMEM((groups * BLOCK, 128), BF16)
    return pl.pallas_call(
        functools.partial(kernel, groups, groups * days_here),
        out_shape=(jax.ShapeDtypeStruct((days_here, pairs, LAGS), BF16), jax.ShapeDtypeStruct((pairs, LAGS), F32)),
        in_specs=[anywhere, vmem, vmem, anywhere],
        out_specs=(vmem, vmem),
        scratch_shapes=[
            pltpu.VMEM((days_here, stations, bins2), BF16),
            pltpu.VMEM((bins2, WIDE), BF16),
            pltpu.VMEM((days_here * pairs, bins2), BF16),
            pltpu.VMEM((groups * BLOCK, 128), F32),
            block, block,
            pltpu.VMEM((groups * 8, 128), F32),
            block, block,
            pltpu.VMEM((groups // ALONG_Y, ALONG_Y * 8, 128), F32),
            padded, padded, padded, padded, padded,
            pltpu.SemaphoreType.DMA,
            pltpu.SemaphoreType.DMA,
            pltpu.SemaphoreType.DMA((9, 2)),
            pltpu.SemaphoreType.DMA((9, 2)),
            pltpu.SemaphoreType.DMA((8,)),
        ],
        compiler_params=pltpu.CompilerParams(
            collective_id=0, has_side_effects=True, vmem_limit_bytes=48 * 2**20),
    )(spectra, pair_stations.T, availability, table)


def solution(mesh):
    return jax.shard_map(
        per_device,
        mesh=mesh,
        in_specs=(P("day", "pair", None), P("pair", None), P("day", None)),
        out_specs=(P("day", "pair", None), P("pair", None)),
        check_vma=False,
    )
```

time: 199 us -> 76.6 us (0.38)
  the two profiles are of different devices: /device:TPU:8 before, /device:TPU:32 now
where the time goes in v2:
time: 76.6 us; the launch traced here: 76.4 us
  Pallas kernels  72 us (94%)
  local copies, waits for them, and re-layouts  3.71 us (5%)
    pallas_call x1, Pallas kernels, per_device(): pl.pallas_call(functools.partial(kernel, groups, groups * days_here), out...  72 us
    unnamed x8, local copies, waits for them, and re-layouts  3.71 us

profile of v2, /device:TPU:32, one launch (start us, length us, event | category | flops | bytes accessed | tf_op | source)
XLA Modules:
  0.0 76.4 jit_solution(5949377200846469192)
XLA Ops:
  0.6 0.0 copy-start
  0.6 0.9 %copy-done = bf16[2,16,4096]{2,1,0:T(8,128)(2,1)S(1)} copy-done((bf16[2,16,4096]{2,1,0:T(8,128)(2,1)S(1)}, bf16[2,16,4096]{2,1,0:T(8,128)(2,1)}, u32[]{:S(2)}) %copy-start) | copy-done | bytes 262168
  1.6 0.0 copy-start.1
  1.6 0.7 copy-done.1
  2.3 0.0 copy-start.2
  2.3 0.7 copy-done.2
  2.9 72.0 %shard_map.59 = (bf16[2,64,1001]{2,1,0:T(8,128)(2,1)S(1)}, f32[64,1001]{1,0:T(8,128)S(1)}) custom-call(bf16[2,16,4096]{2,1,0:T(8,128)(2,1)S(1)} %copy-done, s32[2,64]{1,0:T(2,128)S(1)} %bitcast.1, s32[2,128]{1,0:T(2,128)S(1)} %copy-done.2, bf16[4096,1024]{1,0:T(8,128)(2,1)} %constant.2.clone.table_hbm), custom_call_target="tpu_custom_call" | custom-call | tf_op jit(solution)/shard_map/pallas_call | solution.py:243
  75.0 0.7 copy.8
  75.7 0.7 copy.9
Async XLA Ops:
  0.6 1.0 %copy-start = (bf16[2,16,4096]{2,1,0:T(8,128)(2,1)S(1)}, bf16[2,16,4096]{2,1,0:T(8,128)(2,1)}, u32[]{:S(2)}) copy-start(bf16[2,16,4096]{2,1,0:T(8,128)(2,1)} %spectra.1) | copy-start | bytes 786436
  1.6 0.7 copy-start.1
  2.3 0.7 copy-start.2

commit v3 on v2

v3 whole, which is shorter than its diff:
```python
import functools

import jax
import jax.numpy as jnp
import numpy as np
from jax import lax
from jax.experimental import pallas as pl
from jax.experimental.pallas import tpu as pltpu
from jax.sharding import PartitionSpec as P

LAGS = 1001
WIDE = 1024
TILES = WIDE // 128
WINDOW = 30
ALONG_X = 4
ALONG_Y = 4
BLOCK = 16
PAD = 16
F32 = jnp.float32
BF16 = jnp.bfloat16
MESH = pl.DeviceIdType.MESH
SPOT = LAGS - 128 * (TILES - 1)
VMEM_LIMIT = 58 * 2**20


def lag_table(bin_count):
    bin_ids = np.arange(bin_count)[:, None]
    lag_ids = np.arange(LAGS)[None, :] - (LAGS - 1) // 2
    angle = np.mod(bin_ids * lag_ids, 2 * bin_count) * (np.pi / bin_count)
    factor = 1.0 / np.sqrt(2.0 * bin_count)
    table = np.concatenate([np.cos(angle) * factor, -np.sin(angle) * factor], 0)
    return np.pad(table, ((0, 0), (0, WIDE - LAGS))).astype(np.float32).astype(jnp.bfloat16)


def rows(index, count=BLOCK):
    return pl.ds(pl.multiple_of(index * count, count), count)


def kernel(groups, days, spectra, ends_hbm, availability_hbm, table_hbm, back, refs,
           gathered, table, cross, spread, daily, turned, ready, ends, availability,
           odd_pad, sum_pad, two_pad, four_pad, eight_pad,
           local_sems, give, take, day_sems):
    me = lax.axis_index("day")
    mine = lax.axis_index("pair")
    x, core = mine // 2, mine % 2
    z, y = me // ALONG_Y, me % ALONG_Y
    planes = groups // ALONG_Y
    right = ((x + 1) % ALONG_X) * 2 + core
    left = ((x + ALONG_X - 1) % ALONG_X) * 2 + core
    across = ((x + 2) % ALONG_X) * 2 + core
    sibling = x * 2 + 1 - core
    half = spectra.shape[2] // 2
    pairs = ends.shape[1]
    far = groups // 2

    barrier = pltpu.get_barrier_semaphore()

    def greet(i, carry):
        pl.semaphore_signal(barrier, inc=1, device_id={"day": (me + i) % groups}, device_id_type=MESH)
        return carry

    lax.fori_loop(1, groups, greet, 0)
    for other in (right, left, sibling):
        pl.semaphore_signal(barrier, inc=1, device_id={"pair": other}, device_id_type=MESH)
    own_copy = pltpu.make_async_copy(spectra, gathered.at[:, rows(mine)], local_sems.at[0])
    own_copy.start()
    ends_copy = pltpu.make_async_copy(ends_hbm, ends, local_sems.at[1])
    ends_copy.start()
    availability_copy = pltpu.make_async_copy(availability_hbm, availability, local_sems.at[2])
    availability_copy.start()
    table_copy = pltpu.make_async_copy(table_hbm, table, local_sems.at[3])
    table_copy.start()
    for pad in (odd_pad, sum_pad, two_pad, four_pad, eight_pad):
        pad[0:PAD] = jnp.zeros((PAD, 8, 128), F32)
    pl.semaphore_wait(barrier, groups + 2)

    sent = []

    def to(kind, day, src, dst, other):
        copy = pltpu.make_async_remote_copy(
            src_ref=src, dst_ref=dst, send_sem=give.at[kind, day], recv_sem=take.at[kind, day],
            device_id={"pair": other}, device_id_type=MESH)
        copy.start()
        sent.append(copy)
        return copy

    def block(day, who):
        return gathered.at[day, rows(who)]

    def send_own(day):
        return (to(0, day, spectra.at[day], block(day, mine), right), to(1, day, spectra.at[day], block(day, mine), left),
                to(2, day, spectra.at[day], block(day, mine), sibling))

    def pass_on(day, own):
        part = block(day, left)
        own[0].wait_recv()
        ahead = to(3, day, part.at[:, 0:half], part.at[:, 0:half], right)
        other = block(day, right)
        own[1].wait_recv()
        return (ahead, to(5, day, other.at[:, half:], other.at[:, half:], left),
                to(4, day, part, part, sibling), to(6, day, other, other, sibling))

    def pass_down(day, own, passed):
        part = block(day, across)
        passed[0].wait_recv()
        one = to(7, day, part.at[:, 0:half], part.at[:, 0:half], sibling)
        passed[1].wait_recv()
        two = to(8, day, part.at[:, half:], part.at[:, half:], sibling)
        for copy in (own[2], passed[2], passed[3], one, two):
            copy.wait_recv()

    def cross_of(day):
        width = min(512, half)
        for at in range(0, half, width):
            real = jnp.dot(pick, gathered[day, :, at:at + width], preferred_element_type=F32)
            imag = jnp.dot(pick, gathered[day, :, half + at:half + at + width], preferred_element_type=F32)
            ar, br, ai, bi = real[:pairs], real[pairs:], imag[:pairs], imag[pairs:]
            cross[:, at:at + width] = (ar * br + ai * bi).astype(BF16)
            cross[:, half + at:half + at + width] = (ar * bi - ai * br).astype(BF16)

    def daily_of(day):
        shown = present[day]
        spare = lax.broadcasted_iota(jnp.int32, (pairs, 128), 1) == SPOT
        for at in range(0, WIDE, 256):
            corr = jnp.dot(cross[...], table[:, at:at + 256], preferred_element_type=F32)
            for j in range(2):
                tile = at // 128 + j
                part = corr[:, 128 * j:128 * (j + 1)] * shown
                if tile == TILES - 1:
                    part = jnp.where(spare, shown, part)
                spread[pl.ds(tile, pairs, stride=8), :] = part
        daily[day] = spread[...].reshape(groups, 8, 128).astype(BF16)

    def turn(here, there, send_sem, recv_sem):
        def copy(to_group):
            return pltpu.make_async_remote_copy(
                src_ref=here(to_group, 1), dst_ref=there(me, 1), send_sem=send_sem, recv_sem=recv_sem,
                device_id={"day": to_group}, device_id_type=MESH)

        copy((me + far) % groups).start()

        def step(i, carry):
            copy((me + far + i) % groups).start()
            copy((me + far - i) % groups).start()
            return carry

        lax.fori_loop(1, far, step, 0)
        return pltpu.make_async_remote_copy(
            src_ref=here(0, groups - 1), dst_ref=there(0, groups - 1), send_sem=send_sem, recv_sem=recv_sem,
            device_id={"day": (me + 1) % groups}, device_id_type=MESH)

    def turn_day(day):
        copies = turn(lambda i, n: daily.at[day, pl.ds(i, n)], lambda i, n: turned.at[day, pl.ds(i, n)],
                      day_sems.at[0, day], day_sems.at[1, day])
        turned[day, pl.ds(me, 1)] = daily[day, pl.ds(me, 1)]
        return copies

    own_zero = send_own(0)
    ends_copy.wait()
    availability_copy.wait()
    station = lax.broadcasted_iota(jnp.int32, (128, pairs), 0)
    pick_one = jnp.where(station == ends[0:1, :], 1.0, 0.0).astype(F32).T
    pick_two = jnp.where(station == ends[1:2, :], 1.0, 0.0).astype(F32).T
    pick = jnp.concatenate([pick_one, pick_two], 0).astype(BF16)
    present = []
    for day in range(2):
        up = availability[day:day + 1, :].astype(F32)
        present.append(jnp.sum(pick_one * up, axis=1, keepdims=True) * jnp.sum(pick_two * up, axis=1, keepdims=True))
    own_copy.wait()

    passed_zero = pass_on(0, own_zero)
    own_one = send_own(1)
    pass_down(0, own_zero, passed_zero)
    cross_of(0)
    passed_one = pass_on(1, own_one)
    table_copy.wait()
    daily_of(0)
    turn_zero = turn_day(0)
    pass_down(1, own_one, passed_one)
    cross_of(1)
    daily_of(1)
    turn_one = turn_day(1)
    turn_zero.wait_recv()
    turn_one.wait_recv()

    even, odd = turned[0].astype(F32), turned[1].astype(F32)
    both = even + odd
    ref_row = jnp.sum(both, axis=0) / days
    refs[z, rows(y, 8), :] = ref_row

    def along_z(plane):
        return pltpu.make_async_remote_copy(
            src_ref=refs.at[z, rows(y, 8)], dst_ref=refs.at[z, rows(y, 8)], send_sem=day_sems.at[0, 2], recv_sem=day_sems.at[1, 2],
            device_id={"day": plane * ALONG_Y + y}, device_id_type=MESH)

    def step_z(i, carry):
        along_z((z + i) % planes).start()
        return carry

    lax.fori_loop(1, planes, step_z, 0)
    own = slice(PAD, PAD + groups)

    def past(ref, by):
        return ref[PAD - by:PAD - by + groups]

    odd_pad[own] = odd
    sum_pad[own] = both
    two = both + past(sum_pad, 1)
    two_pad[own] = two
    four = two + past(two_pad, 2)
    four_pad[own] = four
    eight_pad[own] = four + past(four_pad, 4)
    full = past(eight_pad, 1) + past(four_pad, 9) + past(two_pad, 13)
    lag = 128 * lax.broadcasted_iota(jnp.int32, (8, 128), 0) + lax.broadcasted_iota(jnp.int32, (8, 128), 1)
    power = jnp.sum(jnp.where(lag < LAGS, ref_row * ref_row, 0.0), axis=(0, 1), keepdims=True) / LAGS
    scale = jnp.sqrt(power + 1e-06)[None]

    def normalised(moving):
        counts = moving[:, 7:8, SPOT:SPOT + 1]
        return moving * (1.0 / (jnp.maximum(counts, 1.0) * scale))

    ready[...] = jnp.concatenate(
        [normalised(full + past(odd_pad, 15) + even), normalised(full + both)], 1).reshape(groups * BLOCK, 128).astype(BF16)
    home = turn(lambda i, n: ready.at[pl.ds(pl.multiple_of(i * BLOCK, BLOCK), n * BLOCK)],
                lambda i, n: back.at[pl.ds(pl.multiple_of(i * BLOCK, BLOCK), n * BLOCK)],
                day_sems.at[0, 3], day_sems.at[1, 3])
    back[rows(me), :] = ready[rows(me), :]

    got_z = pltpu.make_async_remote_copy(
        src_ref=refs.at[0:planes - 1, 0:8], dst_ref=refs.at[0:planes - 1, 0:8], send_sem=day_sems.at[0, 2], recv_sem=day_sems.at[1, 2],
        device_id={"day": ((z + 1) % planes) * ALONG_Y + y}, device_id_type=MESH)
    got_z.wait_recv()
    for i in range(1, ALONG_Y):
        pltpu.make_async_remote_copy(
            src_ref=refs.at[:, rows(y, 8)], dst_ref=refs.at[:, rows(y, 8)], send_sem=day_sems.at[0, 4], recv_sem=day_sems.at[1, 4],
            device_id={"day": z * ALONG_Y + (y + i) % ALONG_Y}, device_id_type=MESH).start()
    got_y = pltpu.make_async_remote_copy(
        src_ref=refs.at[:, 0:24], dst_ref=refs.at[:, 0:24], send_sem=day_sems.at[0, 4], recv_sem=day_sems.at[1, 4],
        device_id={"day": z * ALONG_Y + (y + 1) % ALONG_Y}, device_id_type=MESH)
    got_y.wait_recv()
    for copy in sent:
        copy.wait_send()
    turn_zero.wait_send()
    turn_one.wait_send()
    got_z.wait_send()
    got_y.wait_send()
    home.wait_recv()
    home.wait_send()


def lay_out(back, refs, stacks_hbm, reference_hbm, spread, held, stacks, reference, sems):
    groups = held.shape[0] // 8
    held[...] = refs[...].reshape(groups * 8, 128)
    for tile in range(TILES):
        wide = min(128, LAGS - 128 * tile)
        reference[:, 128 * tile:128 * tile + wide] = held[pl.ds(tile, groups, stride=8), :][:, :wide]
    copies = [pltpu.make_async_copy(reference, reference_hbm, sems.at[2])]
    copies[0].start()
    spread[...] = back[...].astype(F32)
    for day in range(2):
        for tile in range(TILES):
            wide = min(128, LAGS - 128 * tile)
            part = spread[pl.ds(8 * day + tile, groups, stride=BLOCK), :].astype(BF16)
            stacks[day, :, 128 * tile:128 * tile + wide] = part[:, :wide]
        copies.append(pltpu.make_async_copy(stacks.at[day], stacks_hbm.at[day], sems.at[day]))
        copies[-1].start()
    for copy in copies:
        copy.wait()


def per_device(spectra, pair_stations, availability):
    groups = lax.axis_size("day")
    days_here, shard, bins2 = spectra.shape
    stations = shard * lax.axis_size("pair")
    pairs = pair_stations.shape[0]
    table = jnp.asarray(lag_table(bins2 // 2))
    vmem = pl.BlockSpec(memory_space=pltpu.VMEM)
    anywhere = pl.BlockSpec(memory_space=pl.ANY)
    padded = pltpu.VMEM((PAD + groups, 8, 128), F32)
    by_day = pltpu.VMEM((days_here, groups, 8, 128), BF16)
    dma = pltpu.SemaphoreType.DMA
    back, refs = pl.pallas_call(
        functools.partial(kernel, groups, groups * days_here),
        out_shape=(pltpu.VMEM((groups * BLOCK, 128), BF16),
                   pltpu.VMEM((groups // ALONG_Y, ALONG_Y * 8, 128), F32)),
        in_specs=[anywhere] * 4,
        out_specs=(vmem, vmem),
        scratch_shapes=[
            pltpu.VMEM((days_here, stations, bins2), BF16),
            pltpu.VMEM((bins2, WIDE), BF16),
            pltpu.VMEM((pairs, bins2), BF16),
            pltpu.VMEM((groups * 8, 128), F32),
            by_day, by_day,
            pltpu.VMEM((groups * BLOCK, 128), BF16),
            pltpu.VMEM((2, pairs), jnp.int32),
            pltpu.VMEM((days_here, stations), jnp.int32),
            padded, padded, padded, padded, padded,
            dma((4,)), dma((9, 2)), dma((9, 2)), dma((2, 5)),
        ],
        compiler_params=pltpu.CompilerParams(
            collective_id=0, has_side_effects=True, vmem_limit_bytes=VMEM_LIMIT),
    )(spectra, pair_stations.T, availability, table)
    return pl.pallas_call(
        lay_out,
        out_shape=(jax.ShapeDtypeStruct((days_here, pairs, LAGS), BF16), jax.ShapeDtypeStruct((pairs, LAGS), F32)),
        in_specs=[vmem, vmem],
        out_specs=(anywhere, anywhere),
        scratch_shapes=[
            pltpu.VMEM((groups * BLOCK, 128), F32),
            pltpu.VMEM((groups * 8, 128), F32),
            pltpu.VMEM((days_here, pairs, LAGS), BF16),
            pltpu.VMEM((pairs, LAGS), F32),
            dma((3,)),
        ],
        compiler_params=pltpu.CompilerParams(vmem_limit_bytes=8 * 2**20),
    )(back, refs)


def solution(mesh):
    return jax.shard_map(
        per_device,
        mesh=mesh,
        in_specs=(P("day", "pair", None), P("pair", None), P("day", None)),
        out_specs=(P("day", "pair", None), P("pair", None)),
        check_vma=False,
    )
```

time: 76.6 us -> 65.3 us (0.85)
  the two profiles are of different devices: /device:TPU:32 before, /device:TPU:1 now
where the time goes in v3:
time: 65.3 us; the launch traced here: 64.6 us
  Pallas kernels  63.9 us (98%)
    pallas_call x1, Pallas kernels, per_device(): pl.pallas_call(functools.partial(kernel, groups, groups * days_here), out...  63 us

profile of v3, /device:TPU:1, one launch (start us, length us, event | category | flops | bytes accessed | tf_op | source)
XLA Modules:
  0.0 64.6 jit_solution(2442164779354042685)
XLA Ops:
  0.6 63.0 %shard_map.59 = (bf16[1024,128]{1,0:T(8,128)(2,1)S(1)}, f32[16,32,128]{2,1,0:T(8,128)S(1)}) custom-call(bf16[2,16,4096]{2,1,0:T(8,128)(2,1)} %spectra.1, s32[2,64]{1,0:T(2,128)} %bitcast.1, s32[2,128]{1,0:T(2,128)} %availability_hbm.1, bf16[4096,1024]{1,0:T(8,128)(2,1)} %constant.2.clone.table_hbm), custom_call_target="tpu_custom_call" | custom-call | tf_op jit(solution)/shard_map/pallas_call | solution.py:282
  63.6 1.0 %shard_map.60 = (bf16[2,64,1001]{2,1,0:T(8,128)(2,1)}, f32[64,1001]{1,0:T(8,128)}) custom-call(bf16[1024,128]{1,0:T(8,128)(2,1)S(1)} %get-tuple-element.4.back, f32[16,32,128]{2,1,0:T(8,128)S(1)} %get-tuple-element.5.refs), custom_call_target="tpu_custom_call" | custom-call | tf_op jit(solution)/shard_map/pallas_call | solution.py:303

commit v4 on v3

--- a/solution.py
+++ b/solution.py
@@ -37,7 +37,7 @@
 
 
 def kernel(groups, days, spectra, ends_hbm, availability_hbm, table_hbm, back, refs,
-           gathered, table, cross, spread, daily, turned, ready, ends, availability,
+           gathered, table, cross, handed, spread, daily, turned, ready, ends, availability,
            odd_pad, sum_pad, two_pad, four_pad, eight_pad,
            local_sems, give, take, day_sems):
     me = lax.axis_index("day")
@@ -45,12 +45,10 @@
     x, core = mine // 2, mine % 2
     z, y = me // ALONG_Y, me % ALONG_Y
     planes = groups // ALONG_Y
-    right = ((x + 1) % ALONG_X) * 2 + core
-    left = ((x + ALONG_X - 1) % ALONG_X) * 2 + core
-    across = ((x + 2) % ALONG_X) * 2 + core
     sibling = x * 2 + 1 - core
     half = spectra.shape[2] // 2
-    pairs = ends.shape[1]
+    part = half // 2
+    pairs = ends.shape[2]
     far = groups // 2
 
     barrier = pltpu.get_barrier_semaphore()
@@ -59,12 +57,25 @@
         pl.semaphore_signal(barrier, inc=1, device_id={"day": (me + i) % groups}, device_id_type=MESH)
         return carry
 
+    def at_offset(step, flip):
+        return ((x + step) % ALONG_X) * 2 + (1 - core if flip else core)
+
+    offsets = [(step, flip) for step in (1, 3, 2, 0) for flip in (False, True) if step or flip]
+    for step, flip in offsets:
+        pl.semaphore_signal(barrier, inc=1, device_id={"pair": at_offset(step, flip)}, device_id_type=MESH)
     lax.fori_loop(1, groups, greet, 0)
-    for other in (right, left, sibling):
-        pl.semaphore_signal(barrier, inc=1, device_id={"pair": other}, device_id_type=MESH)
-    own_copy = pltpu.make_async_copy(spectra, gathered.at[:, rows(mine)], local_sems.at[0])
-    own_copy.start()
-    ends_copy = pltpu.make_async_copy(ends_hbm, ends, local_sems.at[1])
+
+    def bins(which, kind):
+        return pl.ds(pl.multiple_of(which * part + kind * half, 128), part)
+
+    own_copies = []
+    for kind in range(2):
+        for day in range(2):
+            own_copies.append(pltpu.make_async_copy(
+                spectra.at[day, :, bins(core, kind)], gathered.at[day, rows(mine), kind * part:(kind + 1) * part],
+                local_sems.at[4 + 2 * kind + day]))
+            own_copies[-1].start()
+    ends_copy = pltpu.make_async_copy(ends_hbm, ends.at[0], local_sems.at[1])
     ends_copy.start()
     availability_copy = pltpu.make_async_copy(availability_hbm, availability, local_sems.at[2])
     availability_copy.start()
@@ -72,63 +83,55 @@
     table_copy.start()
     for pad in (odd_pad, sum_pad, two_pad, four_pad, eight_pad):
         pad[0:PAD] = jnp.zeros((PAD, 8, 128), F32)
-    pl.semaphore_wait(barrier, groups + 2)
+    pl.semaphore_wait(barrier, groups - 1 + len(offsets))
 
     sent = []
 
-    def to(kind, day, src, dst, other):
+    def to(src, dst, send_sem, recv_sem, other):
         copy = pltpu.make_async_remote_copy(
-            src_ref=src, dst_ref=dst, send_sem=give.at[kind, day], recv_sem=take.at[kind, day],
+            src_ref=src, dst_ref=dst, send_sem=send_sem, recv_sem=recv_sem,
             device_id={"pair": other}, device_id_type=MESH)
         copy.start()
         sent.append(copy)
         return copy
 
-    def block(day, who):
-        return gathered.at[day, rows(who)]
-
     def send_own(day):
-        return (to(0, day, spectra.at[day], block(day, mine), right), to(1, day, spectra.at[day], block(day, mine), left),
-                to(2, day, spectra.at[day], block(day, mine), sibling))
-
-    def pass_on(day, own):
-        part = block(day, left)
-        own[0].wait_recv()
-        ahead = to(3, day, part.at[:, 0:half], part.at[:, 0:half], right)
-        other = block(day, right)
-        own[1].wait_recv()
-        return (ahead, to(5, day, other.at[:, half:], other.at[:, half:], left),
-                to(4, day, part, part, sibling), to(6, day, other, other, sibling))
-
-    def pass_down(day, own, passed):
-        part = block(day, across)
-        passed[0].wait_recv()
-        one = to(7, day, part.at[:, 0:half], part.at[:, 0:half], sibling)
-        passed[1].wait_recv()
-        two = to(8, day, part.at[:, half:], part.at[:, half:], sibling)
-        for copy in (own[2], passed[2], passed[3], one, two):
-            copy.wait_recv()
+        copies = []
+        for number, (step, flip) in enumerate(offsets):
+            for kind in range(2):
+                copies.append(to(
+                    spectra.at[day, :, bins(1 - core if flip else core, kind)],
+                    gathered.at[day, rows(mine), kind * part:(kind + 1) * part],
+                    give.at[2 * number + kind, day], take.at[2 * number + kind, day], at_offset(step, flip)))
+        return copies
 
     def cross_of(day):
-        width = min(512, half)
-        for at in range(0, half, width):
+        copies = []
+        width = min(512, part)
+        for number, at in enumerate(range(0, part, width)):
             real = jnp.dot(pick, gathered[day, :, at:at + width], preferred_element_type=F32)
-            imag = jnp.dot(pick, gathered[day, :, half + at:half + at + width], preferred_element_type=F32)
-            ar, br, ai, bi = real[:pairs], real[pairs:], imag[:pairs], imag[pairs:]
-            cross[:, at:at + width] = (ar * br + ai * bi).astype(BF16)
-            cross[:, half + at:half + at + width] = (ar * bi - ai * br).astype(BF16)
+            imag = jnp.dot(pick, gathered[day, :, part + at:part + at + width], preferred_element_type=F32)
+            ar, br, ai, bi = real[:2 * pairs], real[2 * pairs:], imag[:2 * pairs], imag[2 * pairs:]
+            for kind, made in enumerate(((ar * br + ai * bi).astype(BF16), (ar * bi - ai * br).astype(BF16))):
+                place = pl.ds(pl.multiple_of(core * part + kind * half + at, 128), width)
+                handed[day, :, kind * part + at:kind * part + at + width] = made[pairs:]
+                cross[day, :, place] = made[:pairs]
+                copies.append(to(
+                    handed.at[day, :, kind * part + at:kind * part + at + width], cross.at[day, :, place],
+                    give.at[14 + 2 * number + kind, day], take.at[14 + 2 * number + kind, day], sibling))
+        return copies
 
     def daily_of(day):
         shown = present[day]
         spare = lax.broadcasted_iota(jnp.int32, (pairs, 128), 1) == SPOT
         for at in range(0, WIDE, 256):
-            corr = jnp.dot(cross[...], table[:, at:at + 256], preferred_element_type=F32)
+            corr = jnp.dot(cross[day], table[:, at:at + 256], preferred_element_type=F32)
             for j in range(2):
                 tile = at // 128 + j
-                part = corr[:, 128 * j:128 * (j + 1)] * shown
+                piece = corr[:, 128 * j:128 * (j + 1)] * shown
                 if tile == TILES - 1:
-                    part = jnp.where(spare, shown, part)
-                spread[pl.ds(tile, pairs, stride=8), :] = part
+                    piece = jnp.where(spare, shown, piece)
+                spread[pl.ds(tile, pairs, stride=8), :] = piece
         daily[day] = spread[...].reshape(groups, 8, 128).astype(BF16)
 
     def turn(here, there, send_sem, recv_sem):
@@ -157,27 +160,35 @@
 
     own_zero = send_own(0)
     ends_copy.wait()
+    met = to(ends.at[0], ends.at[1], local_sems.at[0], local_sems.at[8], sibling)
+    own_one = send_own(1)
     availability_copy.wait()
+    met.wait_recv()
     station = lax.broadcasted_iota(jnp.int32, (128, pairs), 0)
-    pick_one = jnp.where(station == ends[0:1, :], 1.0, 0.0).astype(F32).T
-    pick_two = jnp.where(station == ends[1:2, :], 1.0, 0.0).astype(F32).T
-    pick = jnp.concatenate([pick_one, pick_two], 0).astype(BF16)
+
+    def picks(end):
+        return [jnp.where(station == ends[who, end:end + 1, :], 1.0, 0.0).astype(F32).T for who in range(2)]
+
+    pick_one, pick_two = picks(0), picks(1)
+    pick = jnp.concatenate(pick_one + pick_two, 0).astype(BF16)
     present = []
     for day in range(2):
         up = availability[day:day + 1, :].astype(F32)
-        present.append(jnp.sum(pick_one * up, axis=1, keepdims=True) * jnp.sum(pick_two * up, axis=1, keepdims=True))
-    own_copy.wait()
-
-    passed_zero = pass_on(0, own_zero)
-    own_one = send_own(1)
-    pass_down(0, own_zero, passed_zero)
-    cross_of(0)
-    passed_one = pass_on(1, own_one)
+        present.append(jnp.sum(pick_one[0] * up, axis=1, keepdims=True) * jnp.sum(pick_two[0] * up, axis=1, keepdims=True))
+    for copy in own_copies:
+        copy.wait()
+    for copy in own_zero:
+        copy.wait_recv()
+    halves_zero = cross_of(0)
     table_copy.wait()
+    for copy in halves_zero:
+        copy.wait_recv()
     daily_of(0)
     turn_zero = turn_day(0)
-    pass_down(1, own_one, passed_one)
-    cross_of(1)
+    for copy in own_one:
+        copy.wait_recv()
+    for copy in cross_of(1):
+        copy.wait_recv()
     daily_of(1)
     turn_one = turn_day(1)
     turn_zero.wait_recv()
@@ -286,16 +297,17 @@
         in_specs=[anywhere] * 4,
         out_specs=(vmem, vmem),
         scratch_shapes=[
-            pltpu.VMEM((days_here, stations, bins2), BF16),
+            pltpu.VMEM((days_here, stations, bins2 // 2), BF16),
             pltpu.VMEM((bins2, WIDE), BF16),
-            pltpu.VMEM((pairs, bins2), BF16),
+            pltpu.VMEM((days_here, pairs, bins2), BF16),
+            pltpu.VMEM((days_here, pairs, bins2 // 2), BF16),
             pltpu.VMEM((groups * 8, 128), F32),
             by_day, by_day,
             pltpu.VMEM((groups * BLOCK, 128), BF16),
-            pltpu.VMEM((2, pairs), jnp.int32),
+            pltpu.VMEM((2, 2, pairs), jnp.int32),
             pltpu.VMEM((days_here, stations), jnp.int32),
             padded, padded, padded, padded, padded,
-            dma((4,)), dma((9, 2)), dma((9, 2)), dma((2, 5)),
+            dma((9,)), dma((18, 2)), dma((18, 2)), dma((2, 5)),
         ],
         compiler_params=pltpu.CompilerParams(
             collective_id=0, has_side_effects=True, vmem_limit_bytes=VMEM_LIMIT),

time: 65.3 us -> 65.3 us (level)
  Pallas kernels: 63.9 us -> 64.6 us
where the time goes in v4:
time: 65.3 us; the launch traced here: 65.2 us
  Pallas kernels  64.6 us (99%)
    pallas_call x1, Pallas kernels, per_device(): pl.pallas_call(functools.partial(kernel, groups, groups * days_here), out...  63.6 us

profile of v4, /device:TPU:1, one launch (start us, length us, event | category | flops | bytes accessed | tf_op | source)
XLA Modules:
  0.0 65.2 jit_solution(7674152183346835677)
XLA Ops:
  0.6 63.6 %shard_map.59 = (bf16[1024,128]{1,0:T(8,128)(2,1)S(1)}, f32[16,32,128]{2,1,0:T(8,128)S(1)}) custom-call(bf16[2,16,4096]{2,1,0:T(8,128)(2,1)} %spectra.1, s32[2,64]{1,0:T(2,128)} %bitcast.1, s32[2,128]{1,0:T(2,128)} %availability_hbm.1, bf16[4096,1024]{1,0:T(8,128)(2,1)} %constant.2.clone.table_hbm), custom_call_target="tpu_custom_call" | custom-call | tf_op jit(solution)/shard_map/pallas_call | solution.py:293
  64.2 1.0 %shard_map.60 = (bf16[2,64,1001]{2,1,0:T(8,128)(2,1)}, f32[64,1001]{1,0:T(8,128)}) custom-call(bf16[1024,128]{1,0:T(8,128)(2,1)S(1)} %get-tuple-element.4.back, f32[16,32,128]{2,1,0:T(8,128)S(1)} %get-tuple-element.5.refs), custom_call_target="tpu_custom_call" | custom-call | tf_op jit(solution)/shard_map/pallas_call | solution.py:315

commit v5 on v4

--- a/solution.py
+++ b/solution.py
@@ -161,7 +161,6 @@
     own_zero = send_own(0)
     ends_copy.wait()
     met = to(ends.at[0], ends.at[1], local_sems.at[0], local_sems.at[8], sibling)
-    own_one = send_own(1)
     availability_copy.wait()
     met.wait_recv()
     station = lax.broadcasted_iota(jnp.int32, (128, pairs), 0)
@@ -175,6 +174,11 @@
     for day in range(2):
         up = availability[day:day + 1, :].astype(F32)
         present.append(jnp.sum(pick_one[0] * up, axis=1, keepdims=True) * jnp.sum(pick_two[0] * up, axis=1, keepdims=True))
+    for copy in own_zero:
+        copy.wait_send()
+    sent.clear()
+    sent.append(met)
+    own_one = send_own(1)
     for copy in own_copies:
         copy.wait()
     for copy in own_zero:
@@ -197,11 +201,11 @@
     even, odd = turned[0].astype(F32), turned[1].astype(F32)
     both = even + odd
     ref_row = jnp.sum(both, axis=0) / days
-    refs[z, rows(y, 8), :] = ref_row
+    refs[pl.ds(z, 1), pl.ds(y, 1)] = ref_row.astype(BF16)[None, None]
 
     def along_z(plane):
         return pltpu.make_async_remote_copy(
-            src_ref=refs.at[z, rows(y, 8)], dst_ref=refs.at[z, rows(y, 8)], send_sem=day_sems.at[0, 2], recv_sem=day_sems.at[1, 2],
+            src_ref=refs.at[pl.ds(z, 1), pl.ds(y, 1)], dst_ref=refs.at[pl.ds(z, 1), pl.ds(y, 1)], send_sem=day_sems.at[0, 2], recv_sem=day_sems.at[1, 2],
             device_id={"day": plane * ALONG_Y + y}, device_id_type=MESH)
 
     def step_z(i, carry):
@@ -238,15 +242,15 @@
     back[rows(me), :] = ready[rows(me), :]
 
     got_z = pltpu.make_async_remote_copy(
-        src_ref=refs.at[0:planes - 1, 0:8], dst_ref=refs.at[0:planes - 1, 0:8], send_sem=day_sems.at[0, 2], recv_sem=day_sems.at[1, 2],
+        src_ref=refs.at[0:planes - 1, 0:1], dst_ref=refs.at[0:planes - 1, 0:1], send_sem=day_sems.at[0, 2], recv_sem=day_sems.at[1, 2],
         device_id={"day": ((z + 1) % planes) * ALONG_Y + y}, device_id_type=MESH)
     got_z.wait_recv()
     for i in range(1, ALONG_Y):
         pltpu.make_async_remote_copy(
-            src_ref=refs.at[:, rows(y, 8)], dst_ref=refs.at[:, rows(y, 8)], send_sem=day_sems.at[0, 4], recv_sem=day_sems.at[1, 4],
+            src_ref=refs.at[:, pl.ds(y, 1)], dst_ref=refs.at[:, pl.ds(y, 1)], send_sem=day_sems.at[0, 4], recv_sem=day_sems.at[1, 4],
             device_id={"day": z * ALONG_Y + (y + i) % ALONG_Y}, device_id_type=MESH).start()
     got_y = pltpu.make_async_remote_copy(
-        src_ref=refs.at[:, 0:24], dst_ref=refs.at[:, 0:24], send_sem=day_sems.at[0, 4], recv_sem=day_sems.at[1, 4],
+        src_ref=refs.at[:, 0:ALONG_Y - 1], dst_ref=refs.at[:, 0:ALONG_Y - 1], send_sem=day_sems.at[0, 4], recv_sem=day_sems.at[1, 4],
         device_id={"day": z * ALONG_Y + (y + 1) % ALONG_Y}, device_id_type=MESH)
     got_y.wait_recv()
     for copy in sent:
@@ -261,7 +265,7 @@
 
 def lay_out(back, refs, stacks_hbm, reference_hbm, spread, held, stacks, reference, sems):
     groups = held.shape[0] // 8
-    held[...] = refs[...].reshape(groups * 8, 128)
+    held[...] = refs[...].astype(F32).reshape(groups * 8, 128)
     for tile in range(TILES):
         wide = min(128, LAGS - 128 * tile)
         reference[:, 128 * tile:128 * tile + wide] = held[pl.ds(tile, groups, stride=8), :][:, :wide]
@@ -293,7 +297,7 @@
     back, refs = pl.pallas_call(
         functools.partial(kernel, groups, groups * days_here),
         out_shape=(pltpu.VMEM((groups * BLOCK, 128), BF16),
-                   pltpu.VMEM((groups // ALONG_Y, ALONG_Y * 8, 128), F32)),
+                   pltpu.VMEM((groups // ALONG_Y, ALONG_Y, 8, 128), BF16)),
         in_specs=[anywhere] * 4,
         out_specs=(vmem, vmem),
         scratch_shapes=[

time: 65.3 us -> 62.2 us (0.953); the launches traced: 65.2 us -> 61.1 us
  Pallas kernels: 64.6 us -> 60.5 us
    pallas_call x1, Pallas kernels: 63.6 us -> 59.5 us  [per_device(): pl.pallas_call(functools.partial(kernel, groups, groups * days_here), out...]
where the time goes in v5:
time: 62.2 us; the launch traced here: 61.1 us
  Pallas kernels  60.5 us (97%)
  between operations  0.64 us (1%)
    pallas_call x1, Pallas kernels, per_device(): pl.pallas_call(functools.partial(kernel, groups, groups * days_here), out...  59.5 us

profile of v5, /device:TPU:1, one launch (start us, length us, event | category | flops | bytes accessed | tf_op | source)
XLA Modules:
  0.0 61.1 jit_solution(17771155375520953464)
XLA Ops:
  0.6 59.5 %shard_map.59 = (bf16[1024,128]{1,0:T(8,128)(2,1)S(1)}, bf16[16,4,8,128]{3,2,1,0:T(8,128)(2,1)S(1)}) custom-call(bf16[2,16,4096]{2,1,0:T(8,128)(2,1)} %spectra.1, s32[2,64]{1,0:T(2,128)} %bitcast.1, s32[2,128]{1,0:T(2,128)} %availability_hbm.1, bf16[4096,1024]{1,0:T(8,128)(2,1)} %constant.2.clone.table_hbm), custom_call_target="tpu_custom_call" | custom-call | tf_op jit(solution)/shard_map/pallas_call | solution.py:297
  60.2 1.0 %shard_map.60 = (bf16[2,64,1001]{2,1,0:T(8,128)(2,1)}, f32[64,1001]{1,0:T(8,128)}) custom-call(bf16[1024,128]{1,0:T(8,128)(2,1)S(1)} %get-tuple-element.4.back, bf16[16,4,8,128]{3,2,1,0:T(8,128)(2,1)S(1)} %get-tuple-element.5.refs), custom_call_target="tpu_custom_call" | custom-call | tf_op jit(solution)/shard_map/pallas_call | solution.py:319

commit v6 on v5

--- a/solution.py
+++ b/solution.py
@@ -37,7 +37,7 @@
 
 
 def kernel(groups, days, spectra, ends_hbm, availability_hbm, table_hbm, back, refs,
-           gathered, table, cross, handed, spread, daily, turned, ready, ends, availability,
+           gathered, table, cross, handed, received, so_far, spread, daily, turned, ready, ends, availability,
            odd_pad, sum_pad, two_pad, four_pad, eight_pad,
            local_sems, give, take, day_sems):
     me = lax.axis_index("day")
@@ -54,8 +54,12 @@
     barrier = pltpu.get_barrier_semaphore()
 
     def greet(i, carry):
-        pl.semaphore_signal(barrier, inc=1, device_id={"day": (me + i) % groups}, device_id_type=MESH)
+        for away in (far + i, far - i):
+            pl.semaphore_signal(barrier, inc=1, device_id={"day": (me + away) % groups}, device_id_type=MESH)
         return carry
+
+    pl.semaphore_signal(barrier, inc=1, device_id={"day": (me + far) % groups}, device_id_type=MESH)
+    lax.fori_loop(1, far // 2, greet, 0)
 
     def at_offset(step, flip):
         return ((x + step) % ALONG_X) * 2 + (1 - core if flip else core)
@@ -63,7 +67,7 @@
     offsets = [(step, flip) for step in (1, 3, 2, 0) for flip in (False, True) if step or flip]
     for step, flip in offsets:
         pl.semaphore_signal(barrier, inc=1, device_id={"pair": at_offset(step, flip)}, device_id_type=MESH)
-    lax.fori_loop(1, groups, greet, 0)
+    lax.fori_loop(far // 2, far, greet, 0)
 
     def bins(which, kind):
         return pl.ds(pl.multiple_of(which * part + kind * half, 128), part)
@@ -79,8 +83,13 @@
     ends_copy.start()
     availability_copy = pltpu.make_async_copy(availability_hbm, availability, local_sems.at[2])
     availability_copy.start()
-    table_copy = pltpu.make_async_copy(table_hbm, table, local_sems.at[3])
-    table_copy.start()
+    table_copies = []
+    for number in range(4):
+        from_row = (core if number < 2 else 1 - core) * part + (number % 2) * half
+        table_copies.append(pltpu.make_async_copy(
+            table_hbm.at[pl.ds(pl.multiple_of(from_row, 128), part)], table.at[number * part:(number + 1) * part],
+            local_sems.at[9 + number]))
+        table_copies[-1].start()
     for pad in (odd_pad, sum_pad, two_pad, four_pad, eight_pad):
         pad[0:PAD] = jnp.zeros((PAD, 8, 128), F32)
     pl.semaphore_wait(barrier, groups - 1 + len(offsets))
@@ -113,19 +122,24 @@
             imag = jnp.dot(pick, gathered[day, :, part + at:part + at + width], preferred_element_type=F32)
             ar, br, ai, bi = real[:2 * pairs], real[2 * pairs:], imag[:2 * pairs], imag[2 * pairs:]
             for kind, made in enumerate(((ar * br + ai * bi).astype(BF16), (ar * bi - ai * br).astype(BF16))):
-                place = pl.ds(pl.multiple_of(core * part + kind * half + at, 128), width)
-                handed[day, :, kind * part + at:kind * part + at + width] = made[pairs:]
+                place = slice(kind * part + at, kind * part + at + width)
+                handed[day, :, place] = made[pairs:]
                 cross[day, :, place] = made[:pairs]
                 copies.append(to(
-                    handed.at[day, :, kind * part + at:kind * part + at + width], cross.at[day, :, place],
+                    handed.at[day, :, place], received.at[day, :, place],
                     give.at[14 + 2 * number + kind, day], take.at[14 + 2 * number + kind, day], sibling))
         return copies
 
-    def daily_of(day):
+    def daily_of(day, copies):
         shown = present[day]
         spare = lax.broadcasted_iota(jnp.int32, (pairs, 128), 1) == SPOT
         for at in range(0, WIDE, 256):
-            corr = jnp.dot(cross[day], table[:, at:at + 256], preferred_element_type=F32)
+            so_far[:, at:at + 256] = jnp.dot(cross[day], table[0:half, at:at + 256], preferred_element_type=F32)
+        for copy in copies:
+            copy.wait_recv()
+        for at in range(0, WIDE, 256):
+            corr = so_far[:, at:at + 256] + jnp.dot(
+                received[day], table[half:2 * half, at:at + 256], preferred_element_type=F32)
             for j in range(2):
                 tile = at // 128 + j
                 piece = corr[:, 128 * j:128 * (j + 1)] * shown
@@ -184,16 +198,13 @@
     for copy in own_zero:
         copy.wait_recv()
     halves_zero = cross_of(0)
-    table_copy.wait()
-    for copy in halves_zero:
-        copy.wait_recv()
-    daily_of(0)
+    for copy in table_copies:
+        copy.wait()
+    daily_of(0, halves_zero)
     turn_zero = turn_day(0)
     for copy in own_one:
         copy.wait_recv()
-    for copy in cross_of(1):
-        copy.wait_recv()
-    daily_of(1)
+    daily_of(1, cross_of(1))
     turn_one = turn_day(1)
     turn_zero.wait_recv()
     turn_one.wait_recv()
@@ -303,15 +314,17 @@
         scratch_shapes=[
             pltpu.VMEM((days_here, stations, bins2 // 2), BF16),
             pltpu.VMEM((bins2, WIDE), BF16),
-            pltpu.VMEM((days_here, pairs, bins2), BF16),
             pltpu.VMEM((days_here, pairs, bins2 // 2), BF16),
+            pltpu.VMEM((days_here, pairs, bins2 // 2), BF16),
+            pltpu.VMEM((days_here, pairs, bins2 // 2), BF16),
+            pltpu.VMEM((pairs, WIDE), F32),
             pltpu.VMEM((groups * 8, 128), F32),
             by_day, by_day,
             pltpu.VMEM((groups * BLOCK, 128), BF16),
             pltpu.VMEM((2, 2, pairs), jnp.int32),
             pltpu.VMEM((days_here, stations), jnp.int32),
             padded, padded, padded, padded, padded,
-            dma((9,)), dma((18, 2)), dma((18, 2)), dma((2, 5)),
+            dma((13,)), dma((18, 2)), dma((18, 2)), dma((2, 5)),
         ],
         compiler_params=pltpu.CompilerParams(
             collective_id=0, has_side_effects=True, vmem_limit_bytes=VMEM_LIMIT),

time: 62.2 us -> 62.4 us (level); the launches traced: 61.1 us -> 62.3 us
  Pallas kernels: 60.5 us -> 61.7 us
    pallas_call x1, Pallas kernels: 59.5 us -> 60.7 us  [per_device(): pl.pallas_call(functools.partial(kernel, groups, groups * days_here), out...]
where the time goes in v6:
time: 62.4 us; the launch traced here: 62.3 us
  Pallas kernels  61.7 us (99%)
  between operations  0.64 us (1%)
    pallas_call x1, Pallas kernels, per_device(): pl.pallas_call(functools.partial(kernel, groups, groups * days_here), out...  60.7 us

profile of v6, /device:TPU:1, one launch (start us, length us, event | category | flops | bytes accessed | tf_op | source)
XLA Modules:
  0.0 62.3 jit_solution(3221122907110981493)
XLA Ops:
  0.6 60.7 %shard_map.59 = (bf16[1024,128]{1,0:T(8,128)(2,1)S(1)}, bf16[16,4,8,128]{3,2,1,0:T(8,128)(2,1)S(1)}) custom-call(bf16[2,16,4096]{2,1,0:T(8,128)(2,1)} %spectra.1, s32[2,64]{1,0:T(2,128)} %bitcast.1, s32[2,128]{1,0:T(2,128)} %availability_hbm.1, bf16[4096,1024]{1,0:T(8,128)(2,1)} %constant.2.clone.table_hbm), custom_call_target="tpu_custom_call" | custom-call | tf_op jit(solution)/shard_map/pallas_call | solution.py:308
  61.4 1.0 %shard_map.60 = (bf16[2,64,1001]{2,1,0:T(8,128)(2,1)}, f32[64,1001]{1,0:T(8,128)}) custom-call(bf16[1024,128]{1,0:T(8,128)(2,1)S(1)} %get-tuple-element.4.back, bf16[16,4,8,128]{3,2,1,0:T(8,128)(2,1)S(1)} %get-tuple-element.5.refs), custom_call_target="tpu_custom_call" | custom-call | tf_op jit(solution)/shard_map/pallas_call | solution.py:332

commit v7 on v6

--- a/solution.py
+++ b/solution.py
@@ -116,7 +116,7 @@
 
     def cross_of(day):
         copies = []
-        width = min(512, part)
+        width = min(1024, part)
         for number, at in enumerate(range(0, part, width)):
             real = jnp.dot(pick, gathered[day, :, at:at + width], preferred_element_type=F32)
             imag = jnp.dot(pick, gathered[day, :, part + at:part + at + width], preferred_element_type=F32)

time: 62.4 us -> 62 us (level)
  no operation moved by 1% of the time
where the time goes in v7:
time: 62 us; the launch traced here: 61.9 us
  Pallas kernels  61.2 us (99%)
  between operations  0.64 us (1%)
    pallas_call x1, Pallas kernels, per_device(): pl.pallas_call(functools.partial(kernel, groups, groups * days_here), out...  60.3 us

profile of v7, /device:TPU:1, one launch (start us, length us, event | category | flops | bytes accessed | tf_op | source)
XLA Modules:
  0.0 61.9 jit_solution(9503743592294954312)
XLA Ops:
  0.6 60.3 %shard_map.59 = (bf16[1024,128]{1,0:T(8,128)(2,1)S(1)}, bf16[16,4,8,128]{3,2,1,0:T(8,128)(2,1)S(1)}) custom-call(bf16[2,16,4096]{2,1,0:T(8,128)(2,1)} %spectra.1, s32[2,64]{1,0:T(2,128)} %bitcast.1, s32[2,128]{1,0:T(2,128)} %availability_hbm.1, bf16[4096,1024]{1,0:T(8,128)(2,1)} %constant.2.clone.table_hbm), custom_call_target="tpu_custom_call" | custom-call | tf_op jit(solution)/shard_map/pallas_call | solution.py:308
  60.9 1.0 %shard_map.60 = (bf16[2,64,1001]{2,1,0:T(8,128)(2,1)}, f32[64,1001]{1,0:T(8,128)}) custom-call(bf16[1024,128]{1,0:T(8,128)(2,1)S(1)} %get-tuple-element.4.back, bf16[16,4,8,128]{3,2,1,0:T(8,128)(2,1)S(1)} %get-tuple-element.5.refs), custom_call_target="tpu_custom_call" | custom-call | tf_op jit(solution)/shard_map/pallas_call | solution.py:332

commit v8 on v7

--- a/solution.py
+++ b/solution.py
@@ -36,9 +36,9 @@
     return pl.ds(pl.multiple_of(index * count, count), count)
 
 
-def kernel(groups, days, spectra, ends_hbm, availability_hbm, table_hbm, back, refs,
+def kernel(groups, days, spectra, ends_hbm, availability_hbm, table_hbm, back, reference,
            gathered, table, cross, handed, received, so_far, spread, daily, turned, ready, ends, availability,
-           odd_pad, sum_pad, two_pad, four_pad, eight_pad,
+           odd_pad, sum_pad, two_pad, four_pad, eight_pad, refs,
            local_sems, give, take, day_sems):
     me = lax.axis_index("day")
     mine = lax.axis_index("pair")
@@ -264,6 +264,10 @@
         src_ref=refs.at[:, 0:ALONG_Y - 1], dst_ref=refs.at[:, 0:ALONG_Y - 1], send_sem=day_sems.at[0, 4], recv_sem=day_sems.at[1, 4],
         device_id={"day": z * ALONG_Y + (y + 1) % ALONG_Y}, device_id_type=MESH)
     got_y.wait_recv()
+    spread[...] = refs[...].astype(F32).reshape(groups * 8, 128)
+    for tile in range(TILES):
+        wide = min(128, LAGS - 128 * tile)
+        reference[:, 128 * tile:128 * tile + wide] = spread[pl.ds(tile, groups, stride=8), :][:, :wide]
     for copy in sent:
         copy.wait_send()
     turn_zero.wait_send()
@@ -274,12 +278,8 @@
     home.wait_send()
 
 
-def lay_out(back, refs, stacks_hbm, reference_hbm, spread, held, stacks, reference, sems):
-    groups = held.shape[0] // 8
-    held[...] = refs[...].astype(F32).reshape(groups * 8, 128)
-    for tile in range(TILES):
-        wide = min(128, LAGS - 128 * tile)
-        reference[:, 128 * tile:128 * tile + wide] = held[pl.ds(tile, groups, stride=8), :][:, :wide]
+def lay_out(back, reference, stacks_hbm, reference_hbm, spread, stacks, sems):
+    groups = back.shape[0] // BLOCK
     copies = [pltpu.make_async_copy(reference, reference_hbm, sems.at[2])]
     copies[0].start()
     spread[...] = back[...].astype(F32)
@@ -305,10 +305,10 @@
     padded = pltpu.VMEM((PAD + groups, 8, 128), F32)
     by_day = pltpu.VMEM((days_here, groups, 8, 128), BF16)
     dma = pltpu.SemaphoreType.DMA
-    back, refs = pl.pallas_call(
+    back, reference = pl.pallas_call(
         functools.partial(kernel, groups, groups * days_here),
         out_shape=(pltpu.VMEM((groups * BLOCK, 128), BF16),
-                   pltpu.VMEM((groups // ALONG_Y, ALONG_Y, 8, 128), BF16)),
+                   pltpu.VMEM((pairs, LAGS), F32)),
         in_specs=[anywhere] * 4,
         out_specs=(vmem, vmem),
         scratch_shapes=[
@@ -324,6 +324,7 @@
             pltpu.VMEM((2, 2, pairs), jnp.int32),
             pltpu.VMEM((days_here, stations), jnp.int32),
             padded, padded, padded, padded, padded,
+            pltpu.VMEM((groups // ALONG_Y, ALONG_Y, 8, 128), BF16),
             dma((13,)), dma((18, 2)), dma((18, 2)), dma((2, 5)),
         ],
         compiler_params=pltpu.CompilerParams(
@@ -336,13 +337,11 @@
         out_specs=(anywhere, anywhere),
         scratch_shapes=[
             pltpu.VMEM((groups * BLOCK, 128), F32),
-            pltpu.VMEM((groups * 8, 128), F32),
             pltpu.VMEM((days_here, pairs, LAGS), BF16),
-            pltpu.VMEM((pairs, LAGS), F32),
             dma((3,)),
         ],
         compiler_params=pltpu.CompilerParams(vmem_limit_bytes=8 * 2**20),
-    )(back, refs)
+    )(back, reference)
 
 
 def solution(mesh):

time: 62 us -> 61.9 us (level)
  no operation moved by 1% of the time
where the time goes in v8:
time: 61.9 us; the launch traced here: 61.8 us
  Pallas kernels  61.2 us (99%)
  between operations  0.64 us (1%)
    pallas_call x1, Pallas kernels, per_device(): pl.pallas_call(functools.partial(kernel, groups, groups * days_here), out...  60.3 us

profile of v8, /device:TPU:1, one launch (start us, length us, event | category | flops | bytes accessed | tf_op | source)
XLA Modules:
  0.0 61.8 jit_solution(3564188150072225408)
XLA Ops:
  0.6 60.3 %shard_map.59 = (bf16[1024,128]{1,0:T(8,128)(2,1)S(1)}, f32[64,1001]{1,0:T(8,128)S(1)}) custom-call(bf16[2,16,4096]{2,1,0:T(8,128)(2,1)} %spectra.1, s32[2,64]{1,0:T(2,128)} %bitcast.1, s32[2,128]{1,0:T(2,128)} %availability_hbm.1, bf16[4096,1024]{1,0:T(8,128)(2,1)} %constant.2.clone.table_hbm), custom_call_target="tpu_custom_call" | custom-call | tf_op jit(solution)/shard_map/pallas_call | solution.py:308
  60.9 0.9 %shard_map.60 = (bf16[2,64,1001]{2,1,0:T(8,128)(2,1)}, f32[64,1001]{1,0:T(8,128)}) custom-call(bf16[1024,128]{1,0:T(8,128)(2,1)S(1)} %get-tuple-element.4.back, f32[64,1001]{1,0:T(8,128)S(1)} %get-tuple-element.5.reference), custom_call_target="tpu_custom_call" | custom-call | tf_op jit(solution)/shard_map/pallas_call | solution.py:333

commit v9 on v8

--- a/solution.py
+++ b/solution.py
@@ -282,13 +282,17 @@
     groups = back.shape[0] // BLOCK
     copies = [pltpu.make_async_copy(reference, reference_hbm, sems.at[2])]
     copies[0].start()
-    spread[...] = back[...].astype(F32)
-    for day in range(2):
-        for tile in range(TILES):
-            wide = min(128, LAGS - 128 * tile)
-            part = spread[pl.ds(8 * day + tile, groups, stride=BLOCK), :].astype(BF16)
-            stacks[day, :, 128 * tile:128 * tile + wide] = part[:, :wide]
-        copies.append(pltpu.make_async_copy(stacks.at[day], stacks_hbm.at[day], sems.at[day]))
+    share = groups // 2
+    for number in range(2):
+        own = slice(number * share, (number + 1) * share)
+        base = number * share * BLOCK
+        spread[base:base + share * BLOCK] = back[base:base + share * BLOCK].astype(F32)
+        for day in range(2):
+            for tile in range(TILES):
+                wide = min(128, LAGS - 128 * tile)
+                part = spread[pl.ds(base + 8 * day + tile, share, stride=BLOCK), :].astype(BF16)
+                stacks[day, own, 128 * tile:128 * tile + wide] = part[:, :wide]
+        copies.append(pltpu.make_async_copy(stacks.at[:, own], stacks_hbm.at[:, own], sems.at[number]))
         copies[-1].start()
     for copy in copies:
         copy.wait()

time: 61.9 us -> 61.9 us (level)
  no operation moved by 1% of the time
where the time goes in v9:
time: 61.9 us; the launch traced here: 61.8 us
  Pallas kernels  61.2 us (99%)
  between operations  0.64 us (1%)
    pallas_call x1, Pallas kernels, per_device(): pl.pallas_call(functools.partial(kernel, groups, groups * days_here), out...  60.3 us

profile of v9, /device:TPU:1, one launch (start us, length us, event | category | flops | bytes accessed | tf_op | source)
XLA Modules:
  0.0 61.8 jit_solution(5517073174667713884)
XLA Ops:
  0.6 60.3 %shard_map.59 = (bf16[1024,128]{1,0:T(8,128)(2,1)S(1)}, f32[64,1001]{1,0:T(8,128)S(1)}) custom-call(bf16[2,16,4096]{2,1,0:T(8,128)(2,1)} %spectra.1, s32[2,64]{1,0:T(2,128)} %bitcast.1, s32[2,128]{1,0:T(2,128)} %availability_hbm.1, bf16[4096,1024]{1,0:T(8,128)(2,1)} %constant.2.clone.table_hbm), custom_call_target="tpu_custom_call" | custom-call | tf_op jit(solution)/shard_map/pallas_call | solution.py:312
  60.9 0.9 %shard_map.60 = (bf16[2,64,1001]{2,1,0:T(8,128)(2,1)}, f32[64,1001]{1,0:T(8,128)}) custom-call(bf16[1024,128]{1,0:T(8,128)(2,1)S(1)} %get-tuple-element.4.back, f32[64,1001]{1,0:T(8,128)S(1)} %get-tuple-element.5.reference), custom_call_target="tpu_custom_call" | custom-call | tf_op jit(solution)/shard_map/pallas_call | solution.py:337
